TPU v7x, 256 devices: a whole 4x4x8 slice. The times are simulated.
256 devices in a mesh: dp: 8 (over z_lo, core), tm: 32 (over x, y, z_hi).
Axes of the slice: x: 4, y: 4, z: 8 (z_hi: 2, z_lo: 4; z = z_hi * 4 + z_lo), core: 2. Of those that a mesh axis runs over, the one named last changes fastest.
Arguments:
- latents: bfloat16 [8, 128, 256, 512], P('dp', 'tm'), may hold values from -6 to 6
- upstream: bfloat16 [8, 128, 256, 512], P('dp', 'tm'), may hold values from -6 to 6
- conv_weight: bfloat16 [3, 512, 512], replicated, may hold values from -0.15625 to 0.15625
- w_query: bfloat16 [512, 512], replicated, may hold values from -20 to 20
- w_key: bfloat16 [512, 512], replicated, may hold values from -1 to 1
- w_value: bfloat16 [512, 512], replicated, may hold values from -0.25 to 0.25
- w_out: bfloat16 [512, 512], replicated, may hold values from -0.25 to 0.25
- norm_gain: float32 [512], replicated, may hold values from 0.1 to 1.9
Outputs:
- grad_latents: bfloat16 [8, 128, 256, 512], P('dp', 'tm')
- grad_conv: float32 [3, 512, 512], P(None, 'tm')
- grad_query: float32 [512, 512], P('tm')
- grad_key: float32 [512, 512], P('tm')
- grad_value: float32 [512, 512], P('tm')
- grad_out: float32 [512, 512], P('tm')
- grad_gain: float32 [512], P('tm')
All inputs are finite; a program needn't handle non-finite values.
Results may differ from a plain program's by a relative error of at most 0.013.
Values may be sent and summed in bfloat16 or wider, within the bound.
A program may use at most 128 MiB of HBM per device.

v0:
```python
import jax
import jax.numpy as jnp
from jax import lax
from jax.sharding import PartitionSpec as P

HEADS = 8


def padded_2(cells, sides, width):
    for axis, dim in sides:
        count = lax.axis_size(axis)
        ends = count - 1
        head = lax.slice_in_dim(cells, 0, width, axis=dim)
        tail = lax.slice_in_dim(cells, cells.shape[dim] - width, cells.shape[dim], axis=dim)
        cells = jnp.concatenate(
            [
                lax.ppermute(tail, axis, [(i, (i + 1) % count) for i in range(ends)]),
                cells,
                lax.ppermute(head, axis, [((i + 1) % count, i) for i in range(ends)]),
            ],
            axis=dim,
        )
    return cells


def cross(left, right):
    return lax.dot_general(
        left, right, (((0,), (0,)), ((), ())), preferred_element_type=jnp.float32
    )


def attend_back(mid, upstream_clip, w_query, w_key, w_value, w_out, norm_gain):
    nframes, npix, width = mid.shape
    shape4 = (nframes, npix, HEADS, width // HEADS)
    scale = (width // HEADS) ** (-0.5)
    upper = mid.reshape(-1, width).astype(jnp.float32)
    rinv = lax.rsqrt(jnp.mean(upper * upper, -1, keepdims=True) + 1e-06)
    normed = (upper * rinv * norm_gain).astype(jnp.bfloat16)
    query = jnp.dot(normed, w_query, preferred_element_type=jnp.float32).astype(jnp.bfloat16)
    keyed = jnp.dot(normed, w_key, preferred_element_type=jnp.float32).astype(jnp.bfloat16)
    valued = jnp.dot(normed, w_value, preferred_element_type=jnp.float32).astype(jnp.bfloat16)
    q4 = query.reshape(shape4)
    k4 = keyed.reshape(shape4)
    v4 = valued.reshape(shape4)
    scores = jnp.einsum("fphd,gphd->phfg", q4, k4, preferred_element_type=jnp.float32) * scale
    probs = jax.nn.softmax(scores, -1)
    probs_b = probs.astype(jnp.bfloat16)
    attended = (
        jnp.einsum("phfg,gphd->fphd", probs_b, v4, preferred_element_type=jnp.float32)
        .astype(jnp.bfloat16)
        .reshape(-1, width)
    )
    flat_up = upstream_clip.reshape(-1, width)
    grad_out = cross(attended, flat_up)
    d_att = jnp.dot(flat_up, w_out.T, preferred_element_type=jnp.float32).astype(jnp.bfloat16)
    da4 = d_att.reshape(shape4)
    d_probs = jnp.einsum("fphd,gphd->phfg", da4, v4, preferred_element_type=jnp.float32)
    d_valued = jnp.einsum(
        "phfg,fphd->gphd", probs_b, da4, preferred_element_type=jnp.float32
    ).astype(jnp.bfloat16)
    d_scores = (probs * (d_probs - jnp.sum(probs * d_probs, -1, keepdims=True)) * scale).astype(
        jnp.bfloat16
    )
    d_query = jnp.einsum(
        "phfg,gphd->fphd", d_scores, k4, preferred_element_type=jnp.float32
    ).astype(jnp.bfloat16)
    d_keyed = jnp.einsum(
        "phfg,fphd->gphd", d_scores, q4, preferred_element_type=jnp.float32
    ).astype(jnp.bfloat16)
    joined = jnp.concatenate(
        [d_query.reshape(-1, width), d_keyed.reshape(-1, width), d_valued.reshape(-1, width)], 1
    )
    weights = jnp.concatenate([w_query, w_key, w_value], 1)
    grads = cross(normed, joined)
    d_normed = jnp.dot(joined, weights.T, preferred_element_type=jnp.float32)
    gain_term = jnp.sum(d_normed * upper * rinv, 0)
    scaled = norm_gain * d_normed
    d_mid = (
        flat_up.astype(jnp.float32)
        + rinv * scaled
        - upper * rinv**3 * jnp.mean(scaled * upper, -1, keepdims=True)
    )
    d_mid = d_mid.astype(jnp.bfloat16).reshape(mid.shape)
    stacked = jnp.stack(
        [grads[:, :width], grads[:, width : 2 * width], grads[:, 2 * width :], grad_out]
    )
    return (d_mid, stacked, gain_term)


def forward_mix(padded, source, conv_weight):
    nframes = source.shape[1]
    width = source.shape[3]
    conv = sum(
        (
            jnp.dot(
                padded[:, k : k + nframes].reshape(-1, width),
                conv_weight[k],
                preferred_element_type=jnp.float32,
            )
            for k in range(3)
        )
    )
    return (
        (source.reshape(-1, width).astype(jnp.float32) + conv)
        .astype(jnp.bfloat16)
        .reshape(source.shape)
    )


def backward_mix(padded, d_mid, grad_pad, conv_weight):
    nframes = d_mid.shape[1]
    width = d_mid.shape[3]
    back = sum(
        (
            jnp.dot(
                grad_pad[:, 2 - k : 2 - k + nframes].reshape(-1, width),
                conv_weight[k].T,
                preferred_element_type=jnp.float32,
            )
            for k in range(3)
        )
    )
    grad_in = (
        (d_mid.reshape(-1, width).astype(jnp.float32) + back)
        .astype(jnp.bfloat16)
        .reshape(d_mid.shape)
    )
    flat_mid = d_mid.reshape(-1, width)
    taps = jnp.stack(
        [cross(padded[:, k : k + nframes].reshape(-1, width), flat_mid) for k in range(3)]
    )
    return (grad_in, taps)


def per_device(latents, upstream, conv_weight, w_query, w_key, w_value, w_out, norm_gain):
    padded = padded_2(latents, (("tm", 1),), 1)
    mid = forward_mix(padded, latents, conv_weight)
    mid_pix, up_pix = (
        lax.all_to_all(mid, "tm", split_axis=2, concat_axis=1, tiled=True),
        lax.all_to_all(upstream, "tm", split_axis=2, concat_axis=1, tiled=True),
    )
    d_mid_pix, stacked, gain_term = attend_back(
        mid_pix[0], up_pix[0], w_query, w_key, w_value, w_out, norm_gain
    )
    d_mid = lax.all_to_all(d_mid_pix[None], "tm", split_axis=1, concat_axis=2, tiled=True)
    grad_pad = padded_2(d_mid, (("tm", 1),), 1)
    grad_in, taps = backward_mix(padded, d_mid, grad_pad, conv_weight)
    terms = jnp.concatenate([taps, stacked], 0)
    rows, gain_rows = (
        lax.psum_scatter(terms, "tm", scatter_dimension=1, tiled=True),
        lax.psum_scatter(gain_term, "tm", scatter_dimension=0, tiled=True),
    )
    rows, gain_rows = lax.psum((rows, gain_rows), "dp")
    return (grad_in, rows[0:3], rows[3], rows[4], rows[5], rows[6], gain_rows)


def solution(mesh):
    return jax.shard_map(
        per_device,
        mesh=mesh,
        in_specs=(
            P("dp", "tm", None, None),
            P("dp", "tm", None, None),
            P(),
            P(),
            P(),
            P(),
            P(),
            P(),
        ),
        out_specs=(
            P("dp", "tm", None, None),
            P(None, "tm", None),
            P("tm", None),
            P("tm", None),
            P("tm", None),
            P("tm", None),
            P("tm"),
        ),
        check_vma=False,
    )
```

profile of v0, /device:TPU:1, one launch (start us, length us, event | category | flops | bytes accessed | tf_op | source)
XLA Modules:
  0.0 691.7 jit_solution(13309821000457990153)
XLA Ops:
  7.2 3.2 copy.101
  10.4 14.6 %all-to-all-start = ((bf16[1,4,256,512]{3,1,0,2:T(4,128)(2,1)}), bf16[1,4,256,512]{3,1,0,2:T(4,128)(2,1)}, u32[]{:S(2)}, u32[]{:S(2)}) async-start(bf16[1,4,256,512]{3,1,0,2:T(4,128)(2,1)} %copy.101), calls=%async_computation | async-start | bytes 2097152 | tf_op jit(solution)/shard_map/all_to_all | solution.py:140
  26.4 7.9 %collective-permute-start = (bf16[1,1,256,512]{3,2,1,0:T(8,128)(2,1)S(1)}, bf16[1,1,256,512]{3,2,1,0:T(8,128)(2,1)S(1)}, u32[]{:S(2)}, u32[]{:S(2)}) collective-permute-start(bf16[1,1,256,512]{3,2,1,0:T(8,128)(2,1)S(1)} %get-tuple-element.18), channel_id=1, source_target_pairs={{0,1},{1,2},{2,3},{3,4},{4,5},{5,6},{6,7},{7,8},{8,9},{9,10},{10,1... | collective-permute-start | bytes 786440 | tf_op jit(solution)/shard_map/ppermute | solution.py:17
  35.0 15.3 %collective-permute-done.1 = bf16[1,1,256,512]{3,2,1,0:T(8,128)(2,1)S(1)} collective-permute-done((bf16[1,1,256,512]{3,2,1,0:T(8,128)(2,1)S(1)}, bf16[1,1,256,512]{3,2,1,0:T(8,128)(2,1)S(1)}, u32[]{:S(2)}, u32[]{:S(2)}) %collective-permute-start.1) | collective-permute-done | bytes 262176 | tf_op jit(solution)/shard_map/ppermute | solution.py:19
  52.2 1.8 copy.103
  54.0 26.4 %all-to-all-start.1 = ((bf16[1,4,256,512]{3,1,0,2:T(4,128)(2,1)}), bf16[1,4,256,512]{3,1,0,2:T(4,128)(2,1)S(1)}, u32[]{:S(2)}, u32[]{:S(2)}) async-start(bf16[1,4,256,512]{3,1,0,2:T(4,128)(2,1)} %copy.103), calls=%async_computation.1 | async-start | bytes 2097152 | tf_op jit(solution)/shard_map/all_to_all | solution.py:139
  82.9 1.7 convolution_convert_fusion.3
  84.6 3.9 reshape.117
  88.5 4.0 copy.109
  92.5 5.0 all-to-all-done.1
  103.0 3.9 reshape.118
  106.9 4.1 copy.110
  111.0 3.0 convolution_convert_fusion.4
  114.0 3.9 reshape.116
  117.9 4.0 copy.107
  121.9 3.0 convolution_convert_fusion.5
  125.0 3.9 reshape.115
  128.9 4.2 copy.111
  133.1 4.3 fusion.89
  137.3 5.1 fusion.87
  142.5 5.0 fusion.37
  147.5 8.5 %fusion.43 = bf16[128,8,8,64]{0,3,2,1:T(8,128)(2,1)} fusion(bf16[128,8,8,64]{0,3,2,1:T(8,128)(2,1)} %copy.107, f32[8,8,128,128]{2,3,1,0:T(8,128)} %fusion.89, f32[8,8,128,128]{2,3,1,0:T(8,128)} %get-tuple-element.24, f32[8,8,128]{2,1,0:T(8,128)S(1)} %get-tuple-element.23), kind=kOutput, calls=%fused_computation.53 | convolution fusion | flops 142090368 | bytes 10518528 | tf_op jit(solution)/shard_map/phfg,fphd->gphd/dot_general | solution.py:67
  156.0 8.5 %fusion.46 = bf16[128,8,8,64]{0,3,2,1:T(8,128)(2,1)} fusion(bf16[128,8,8,64]{0,3,2,1:T(8,128)(2,1)} %copy.111, f32[8,8,128,128]{2,3,1,0:T(8,128)} %fusion.89, f32[8,8,128,128]{2,3,1,0:T(8,128)} %get-tuple-element.24, f32[8,8,128]{2,1,0:T(8,128)S(1)} %get-tuple-element.23), kind=kOutput, calls=%fused_computation.54 | convolution fusion | flops 142090368 | bytes 10518528 | tf_op jit(solution)/shard_map/phfg,gphd->fphd/dot_general | solution.py:64
  164.5 4.8 copy.113
  169.2 4.1 reshape.119
  173.3 4.8 copy.116
  178.0 4.0 reshape.120
  182.1 4.8 copy.119
  186.8 4.3 reshape.121
  194.0 2.1 fusion.21
  197.7 6.9 %all-to-all-start.2 = ((bf16[1,128,8,512]{3,2,0,1:T(8,128)(2,1)}), bf16[1,128,8,512]{3,2,0,1:T(8,128)(2,1)}, u32[]{:S(2)}, u32[]{:S(2)}) async-start(bf16[1,128,8,512]{3,2,0,1:T(8,128)(2,1)} %bitcast.180), calls=%async_computation.2 | async-start | bytes 2097152 | tf_op jit(solution)/shard_map/all_to_all | solution.py:145
  204.6 4.2 fusion.38
  208.9 3.9 copy.125
  212.8 2.0 reshape.126
  214.8 5.7 fusion.90
  222.3 2.9 fusion.42
  225.2 1.8 fusion.41
  227.0 1.7 fusion.40
  232.4 1.7 fusion.39
  236.1 119.1 %all-reduce = f32[512]{0:T(512)S(1)} all-reduce(f32[512]{0:T(512)S(1)} %get-tuple-element.7), channel_id=3, replica_groups=mesh['dp'=8,'tm'=32] {'tm'}, use_global_device_ids=true, to_apply=%region_8.0.clone | all-reduce | flops 512 | bytes 4096
  355.2 42.0 %psum.15 = f32[16]{0:T(128)} all-reduce(f32[16]{0:T(128)S(1)} %dynamic-slice.1), channel_id=1, replica_groups=mesh['dp'=8,'tm'=32] {'dp'}, use_global_device_ids=true, to_apply=%region_9.0 | all-reduce | flops 16 | bytes 128 | tf_op jit(solution)/shard_map/psum | solution.py:153
  400.0 2.0 fusion.62
  402.0 22.3 %collective-permute-done.3 = bf16[1,1,256,512]{3,2,1,0:T(8,128)(2,1)S(1)} collective-permute-done((bf16[1,1,256,512]{3,2,1,0:T(8,128)(2,1)S(1)}, bf16[1,1,256,512]{3,2,1,0:T(8,128)(2,1)S(1)}, u32[]{:S(2)}, u32[]{:S(2)}) %collective-permute-start.3) | collective-permute-done | bytes 262176 | tf_op jit(solution)/shard_map/ppermute | solution.py:17
  424.3 19.3 %collective-permute-done.2 = bf16[1,1,256,512]{3,2,1,0:T(8,128)(2,1)S(1)} collective-permute-done((bf16[1,1,256,512]{3,2,1,0:T(8,128)(2,1)S(1)}, bf16[1,1,256,512]{3,2,1,0:T(8,128)(2,1)S(1)}, u32[]{:S(2)}, u32[]{:S(2)}) %collective-permute-start.2) | collective-permute-done | bytes 262176 | tf_op jit(solution)/shard_map/ppermute | solution.py:19
  444.8 2.1 fusion.66
  447.0 163.5 %reduce-scatter.2.cloned.1.call-done = f32[7,16,512]{2,1,0:T(8,128)} async-done(((f32[7,512,512]{2,1,0:T(8,128)}), f32[7,16,512]{2,1,0:T(8,128)}) %reduce-scatter.2.cloned.1.call-update) | async-done | bytes 229392 | tf_op jit(solution)/shard_map/reduce_scatter | solution.py:150
  610.4 4.4 add_convert_fusion
  614.8 66.8 %all-reduce.3.cloned.1.call-done = f32[7,16,512]{2,1,0:T(8,128)} async-done(((f32[7,16,512]{2,1,0:T(8,128)}), f32[7,16,512]{2,1,0:T(8,128)}) %all-reduce.3.cloned.1.call-update) | async-done | bytes 229392 | tf_op jit(solution)/shard_map/psum | solution.py:153
  (85 shorter events, 30.0 us)
Async XLA Ops:
  7.2 75.7 %copy-start = (bf16[512,512]{1,0:T(8,128)(2,1)S(1)}, bf16[512,512]{1,0:T(8,128)(2,1)}, u32[]{:S(2)}) copy-start(bf16[512,512]{1,0:T(8,128)(2,1)} %param.14) | copy-start | bytes 1572868
  7.2 17.8 %copy-start.2 = (bf16[1,4,256,512]{3,2,1,0:T(8,128)(2,1)S(1)}, bf16[1,4,256,512]{3,2,1,0:T(8,128)(2,1)}, u32[]{:S(2)}) copy-start(bf16[1,4,256,512]{3,2,1,0:T(8,128)(2,1)} %param.8) | copy-start | bytes 3145732
  7.2 27.1 %copy-start.4 = (bf16[3,512,512]{2,1,0:T(8,128)(2,1)S(1)}, bf16[3,512,512]{2,1,0:T(8,128)(2,1)}, u32[]{:S(2)}) copy-start(bf16[3,512,512]{2,1,0:T(8,128)(2,1)} %param.10) | copy-start | bytes 4718596
  10.4 43.6 %all-to-all-start = ((bf16[1,4,256,512]{3,1,0,2:T(4,128)(2,1)}), bf16[1,4,256,512]{3,1,0,2:T(4,128)(2,1)}, u32[]{:S(2)}, u32[]{:S(2)}) async-start(bf16[1,4,256,512]{3,1,0,2:T(4,128)(2,1)} %copy.101), calls=%async_computation | async-start | bytes 2097152 | tf_op jit(solution)/shard_map/all_to_all | solution.py:140
  25.1 25.3 %collective-permute-start.1 = (bf16[1,1,256,512]{3,2,1,0:T(8,128)(2,1)S(1)}, bf16[1,1,256,512]{3,2,1,0:T(8,128)(2,1)S(1)}, u32[]{:S(2)}, u32[]{:S(2)}) collective-permute-start(bf16[1,1,256,512]{3,2,1,0:T(8,128)(2,1)S(1)} %get-tuple-element.17), channel_id=1, source_target_pairs={{1,0},{2,1},{3,2},{4,3},{5,4},{6,5},{7,6},{8,7},{9,8},{10,9},{11,1... | collective-permute-start | bytes 786440 | tf_op jit(solution)/shard_map/ppermute | solution.py:19
  26.4 24.0 %collective-permute-start = (bf16[1,1,256,512]{3,2,1,0:T(8,128)(2,1)S(1)}, bf16[1,1,256,512]{3,2,1,0:T(8,128)(2,1)S(1)}, u32[]{:S(2)}, u32[]{:S(2)}) collective-permute-start(bf16[1,1,256,512]{3,2,1,0:T(8,128)(2,1)S(1)} %get-tuple-element.18), channel_id=1, source_target_pairs={{0,1},{1,2},{2,3},{3,4},{4,5},{5,6},{6,7},{7,8},{8,9},{9,10},{10,1... | collective-permute-start | bytes 786440 | tf_op jit(solution)/shard_map/ppermute | solution.py:17
  50.5 1.7 copy-start.6
  50.5 1.7 copy-start.8
  54.0 43.5 %all-to-all-start.1 = ((bf16[1,4,256,512]{3,1,0,2:T(4,128)(2,1)}), bf16[1,4,256,512]{3,1,0,2:T(4,128)(2,1)S(1)}, u32[]{:S(2)}, u32[]{:S(2)}) async-start(bf16[1,4,256,512]{3,1,0,2:T(4,128)(2,1)} %copy.103), calls=%async_computation.1 | async-start | bytes 2097152 | tf_op jit(solution)/shard_map/all_to_all | solution.py:139
  81.9 1.0 copy-start.9
  92.5 7.6 %copy-start.17 = (f32[512]{0:T(512)S(1)}, f32[512]{0:T(512)}, u32[]{:S(2)}) copy-start(f32[512]{0:T(512)} %param.15) | copy-start | bytes 6148
  97.5 1.0 copy-start.3
  98.5 2.8 copy-start.19
  100.4 1.0 copy-start.15
  191.1 2.8 copy-start.12
  191.1 2.8 copy-start.18
  191.1 2.9 copy-start.20
  191.1 2.9 copy-start.21
  194.0 2.1 copy-start.16
  194.0 2.1 copy-start.10
  197.7 23.3 %all-to-all-start.2 = ((bf16[1,128,8,512]{3,2,0,1:T(8,128)(2,1)}), bf16[1,128,8,512]{3,2,0,1:T(8,128)(2,1)}, u32[]{:S(2)}, u32[]{:S(2)}) async-start(bf16[1,128,8,512]{3,2,0,1:T(8,128)(2,1)} %bitcast.180), calls=%async_computation.2 | async-start | bytes 2097152 | tf_op jit(solution)/shard_map/all_to_all | solution.py:145
  204.6 405.8 %reduce-scatter.2.cloned.1.call-start = ((), (), s32[]{:S(2)}) async-start(), calls=%async_computation.4 | async-start | bytes 7569408 | tf_op jit(solution)/shard_map/reduce_scatter | solution.py:150
  225.2 1.8 copy-start.7
  227.0 2.3 copy-start.13
  229.2 3.2 copy-start.11
  229.2 3.2 copy-start.14
  234.2 0.7 copy-start.22
  234.2 165.8 %copy-start.5 = (bf16[3,512,512]{2,1,0:T(8,128)(2,1)S(1)}, bf16[3,512,512]{2,1,0:T(8,128)(2,1)}, u32[]{:S(2)}) copy-start(bf16[3,512,512]{2,1,0:T(8,128)(2,1)} %param.10) | copy-start | bytes 4718596
  234.2 447.4 %all-reduce.3.cloned.1.call-start = ((), (), s32[]{:S(2)}) async-start(), calls=%async_computation.5 | async-start | bytes 458752 | tf_op jit(solution)/shard_map/psum | solution.py:153
  397.3 27.0 %collective-permute-start.3 = (bf16[1,1,256,512]{3,2,1,0:T(8,128)(2,1)S(1)}, bf16[1,1,256,512]{3,2,1,0:T(8,128)(2,1)S(1)}, u32[]{:S(2)}, u32[]{:S(2)}) collective-permute-start(bf16[1,1,256,512]{3,2,1,0:T(8,128)(2,1)S(1)} %get-tuple-element.11), channel_id=1, source_target_pairs={{0,1},{1,2},{2,3},{3,4},{4,5},{5,6},{6,7},{7,8},{8,9},{9,10},{10,1... | collective-permute-start | bytes 786440 | tf_op jit(solution)/shard_map/ppermute | solution.py:17
  398.7 44.9 %collective-permute-start.2 = (bf16[1,1,256,512]{3,2,1,0:T(8,128)(2,1)S(1)}, bf16[1,1,256,512]{3,2,1,0:T(8,128)(2,1)S(1)}, u32[]{:S(2)}, u32[]{:S(2)}) collective-permute-start(bf16[1,1,256,512]{3,2,1,0:T(8,128)(2,1)S(1)} %get-tuple-element.12), channel_id=1, source_target_pairs={{1,0},{2,1},{3,2},{4,3},{5,4},{6,5},{7,6},{8,7},{9,8},{10,9},{11,1... | collective-permute-start | bytes 786440 | tf_op jit(solution)/shard_map/ppermute | solution.py:19
  610.4 74.2 %copy-start.1 = (bf16[512,512]{1,0:T(8,128)(2,1)S(1)}, bf16[512,512]{1,0:T(8,128)(2,1)}, u32[]{:S(2)}) copy-start(bf16[512,512]{1,0:T(8,128)(2,1)} %param.14) | copy-start | bytes 1572868
Sparse Core Ops, SparseCore 0:
  234.3 376.0 reduce-scatter.1
  613.0 68.5 all-reduce.2
where the time goes:
time: 697 us; the launch traced here: 692 us
  waiting for transfers between devices  293 us (42%)
  blocking collectives  161 us (23%)
  local copies, waits for them, and re-layouts  87.1 us (12%)
  matrix products  71.9 us (10%)
  starting transfers between devices  59.9 us (9%)
  between operations  15.3 us (2%)
    reduce_scatter x1, waiting for transfers between devices, per_device(): lax.psum_scatter(terms, 'tm', scatter_dimension=1, tiled=True)  163 us
    unnamed x1, blocking collectives  119 us
    psum x1, waiting for transfers between devices, per_device(): rows, gain_rows = lax.psum((rows, gain_rows), 'dp')  66.8 us
    psum x1, blocking collectives, per_device(): rows, gain_rows = lax.psum((rows, gain_rows), 'dp')  42 us
    ppermute x2, waiting for transfers between devices, padded_2(): lax.ppermute(head, axis, [((i + 1) % count, i) for i in range(ends)])  34.6 us
    all_to_all x1, starting transfers between devices, per_device(): lax.all_to_all(mid, 'tm', split_axis=2, concat_axis=1, tiled=True)  26.4 us
    ppermute x2, waiting for transfers between devices, padded_2(): lax.ppermute(tail, axis, [(i, (i + 1) % count) for i in range(ends)])  22.3 us
    all_to_all x1, starting transfers between devices, per_device(): lax.all_to_all(upstream, 'tm', split_axis=2, concat_axis=1, tiled=True)  14.6 us
  transfers between devices with their start and end apart: 9, of which 7 were waited for; matrix products, arithmetic and copies ran while one was open for 6% of the time, Pallas kernels for 0%

commit v1 on v0

v1 whole, which is shorter than its diff:
```python
import jax
import jax.numpy as jnp
from jax import lax
from jax.experimental import pallas as pl
from jax.experimental.pallas import tpu as pltpu
from jax.sharding import PartitionSpec as P

C = 512
F = 128
TM = 32
BF = jnp.bfloat16
F32 = jnp.float32
MESH_ID = pl.DeviceIdType.MESH


def nn(a, b):
    return lax.dot_general(a, b, (((1,), (0,)), ((), ())), preferred_element_type=F32)


def nt(a, b):
    return lax.dot_general(a, b, (((1,), (1,)), ((), ())), preferred_element_type=F32)


def tn(a, b):
    return lax.dot_general(a, b, (((0,), (0,)), ((), ())), preferred_element_type=F32)


def where_am_i():
    dp, tm = lax.axis_index("dp"), lax.axis_index("tm")
    return dict(dp=dp, tm=tm, zl=dp // 2, c=dp % 2, x=tm // 8, y=(tm // 2) % 4, zh=tm % 2)


def device(zl, c, x, y, zh):
    return {"dp": zl * 2 + c, "tm": (x * 4 + y) * 2 + zh}


def signal(sem, dev):
    pl.semaphore_signal(sem, inc=1, device_id=dev, device_id_type=MESH_ID)


def send(src, dst, ssem, rsem, dev):
    pltpu.make_async_remote_copy(
        src_ref=src, dst_ref=dst, send_sem=ssem, recv_sem=rsem,
        device_id=dev, device_id_type=MESH_ID,
    ).start()


def wait_bytes(ref, sem):
    pltpu.make_async_copy(ref, ref, sem).wait()


def row_of(shape):
    return lax.broadcasted_iota(jnp.int32, shape, 0)


def split_heads(a):
    lane = lax.broadcasted_iota(jnp.int32, a.shape, 1)
    zero = jnp.zeros_like(a)
    return jnp.concatenate([jnp.where(lane < 64, a, zero), jnp.where(lane < 64, zero, a)], 0)


def join_heads(a):
    lane = lax.broadcasted_iota(jnp.int32, (F, 128), 1)
    return jnp.where(lane < 64, a[:F], a[F:])


def kernel(
    lat, up, wc, wq, wk, wv, wo, gain,
    out, ograds, ogain,
    sbl, sbu, rl, ru, osend, orecv,
    t32, x_s, mid_s, nrm_s, qkv_s, pr_s, att_s, up_s, da_s, dqkv_s, dm_s,
    g_s, gain_s, g0s_a, g0s_b, g0r_a, g0r_b,
    s1_a, r1_a, s2_a, r2_a, s1_b, r1_b, s2_b, r2_b,
    t_s, zr, zsum, agr, gn_s, gn0, gnx, gny, gnz,
    ssem, rsem,
):
    w = where_am_i()
    me, c, x, y, zl, zh = w["tm"], w["c"], w["x"], w["y"], w["zl"], w["zh"]
    z = zh * 4 + zl

    def at_z(zz, cc):
        return device(zz % 4, cc, x, y, zz // 4)

    barrier = pltpu.get_barrier_semaphore()

    @pl.loop(1, TM)
    def _(k):
        signal(barrier, {"dp": w["dp"], "tm": (me + k) % TM})

    signal(barrier, device(zl, 1 - c, x, y, zh))

    @pl.loop(1, 8)
    def _(k):
        @pl.when(k != 4)
        def _():
            signal(barrier, at_z((z + k) % 8, c))

    @pl.loop(1, 4)
    def _(k):
        signal(barrier, at_z(zh * 4 + (zl + k) % 4, 1 - c))

    def regroup(src, dst, h):
        a = [src[f, 128 * h:128 * h + 128, :].astype(F32) for f in range(4)]
        low = row_of((F, C)) % 8 < 4
        tiles = []
        for f in (0, 2):
            even = jnp.where(low, a[f], pltpu.roll(a[f + 1], 4, 0))
            odd = jnp.where(low, pltpu.roll(a[f], F - 4, 0), a[f + 1])
            tiles.append((even.reshape(16, 8, C), odd.reshape(16, 8, C)))
        for m in range(16):
            for o in range(2):
                dst[h, 2 * m + o] = jnp.concatenate(
                    [tiles[0][o][m], tiles[1][o][m]], 0
                ).astype(BF)

    def scatter(src, dst, h, i):
        @pl.loop(1, TM)
        def _(k):
            to = (me + k) % TM
            send(src.at[h, to], dst.at[h, me], ssem.at[i], rsem.at[i],
                 {"dp": w["dp"], "tm": to})
        dst[h, me] = src[h, me]

    def arrived(dst, h, i):
        wait_bytes(dst.at[h, pl.ds(0, TM - 1)], rsem.at[i])

    regroup(lat, sbl, 0)
    regroup(lat, sbl, 1)
    pl.semaphore_wait(barrier, 41)
    scatter(sbl, rl, 0, 0)
    scatter(sbl, rl, 1, 1)
    regroup(up, sbu, 0)
    regroup(up, sbu, 1)

    def by_pixel(src, dst, h):
        wide = src[h].reshape(512, C).astype(F32)
        for i in range(4):
            t32[i] = wide[:, i * 128:i * 128 + 128]
        for p in range(4):
            for i in range(4):
                dst[pl.ds(h * 512 + p * F, F), i * 128:i * 128 + 128] = (
                    t32[i, pl.ds(p, F, stride=4), :].astype(BF))

    def forward_dense(h):
        base = h * 512
        rows = pl.ds(base, 512)
        by_pixel(rl, x_s, h)
        xx = x_s[rows, :]
        frame = row_of((512, C)) % F
        conv = jnp.where(frame == 0, 0.0, pltpu.roll(nn(xx, wc[0]), 1, 0))
        conv = conv + nn(xx, wc[1])
        conv = conv + jnp.where(frame == F - 1, 0.0, pltpu.roll(nn(xx, wc[2]), 511, 0))
        mid = (xx.astype(F32) + conv).astype(BF)
        mid_s[rows, :] = mid
        upper = mid.astype(F32)
        rinv = lax.rsqrt(jnp.mean(upper * upper, -1, keepdims=True) + 1e-06)
        normed = (upper * rinv * gain[...]).astype(BF)
        nrm_s[rows, :] = normed
        for i, weight in enumerate((wq, wk, wv)):
            qkv_s[rows, i * C:(i + 1) * C] = nn(normed, weight[...]).astype(BF)

    def forward_attend(p):
        rows = pl.ds(pl.multiple_of(p * F, F), F)
        for j in range(4):
            q = qkv_s[rows, j * 128:j * 128 + 128]
            k2 = split_heads(qkv_s[rows, C + j * 128:C + j * 128 + 128])
            v2 = split_heads(qkv_s[rows, 2 * C + j * 128:2 * C + j * 128 + 128])
            s = (nt(k2, q) * 0.125).reshape(2, F, F)
            e = jnp.exp(s - jnp.max(s, 1, keepdims=True))
            probs = (e / jnp.sum(e, 1, keepdims=True)).reshape(2 * F, F)
            pr_s[p * 4 + j] = probs
            att_s[rows, j * 128:j * 128 + 128] = tn(probs.astype(BF), v2).astype(BF)

    for h in range(2):
        arrived(rl, h, h)
        if h == 0:
            scatter(sbu, ru, 0, 2)
        forward_dense(h)
        if h == 1:
            scatter(sbu, ru, 1, 3)

        @pl.loop(4 * h, 4 * h + 4)
        def _(p):
            forward_attend(p)

    def backward_att(h):
        base = h * 512
        rows = pl.ds(base, 512)
        by_pixel(ru, up_s, h)
        da_s[rows, :] = nt(up_s[rows, :], wo[...]).astype(BF)

    def backward_attend(p):
        rows = pl.ds(pl.multiple_of(p * F, F), F)
        for j in range(4):
            lanes = slice(j * 128, j * 128 + 128)
            q = qkv_s[rows, j * 128:j * 128 + 128]
            k2 = split_heads(qkv_s[rows, C + j * 128:C + j * 128 + 128])
            v2 = split_heads(qkv_s[rows, 2 * C + j * 128:2 * C + j * 128 + 128])
            da = da_s[rows, lanes]
            probs = pr_s[p * 4 + j]
            dp = nt(v2, da)
            dv = join_heads(nn(probs.astype(BF), da))
            p3, d3 = probs.reshape(2, F, F), dp.reshape(2, F, F)
            ds = p3 * (d3 - jnp.sum(p3 * d3, 1, keepdims=True)) * 0.125
            ds = ds.reshape(2 * F, F).astype(BF)
            dqkv_s[rows, j * 128:j * 128 + 128] = tn(ds, k2).astype(BF)
            dqkv_s[rows, C + j * 128:C + j * 128 + 128] = join_heads(nn(ds, q)).astype(BF)
            dqkv_s[rows, 2 * C + j * 128:2 * C + j * 128 + 128] = dv.astype(BF)

    def put(i, h, value):
        value = value.reshape(16, 2, 16, C)
        if h == 0:
            g_s[i] = value
        else:
            g_s[i] = g_s[i] + value

    def grads_first(h):
        rows = pl.ds(h * 512, 512)
        put(6, h, tn(att_s[rows, :], up_s[rows, :]))
        for i in range(3):
            put(3 + i, h, tn(nrm_s[rows, :], dqkv_s[rows, i * C:(i + 1) * C]))

    def grads_taps(h):
        rows = pl.ds(h * 512, 512)
        for i in range(3):
            put(i, h, tn(x_s[rows, :], dm_s[rows, i * C:(i + 1) * C]))

    def backward_dense(h):
        base = h * 512
        rows = pl.ds(base, 512)
        d_normed = nt(dqkv_s[rows, 0:C], wq[...])
        d_normed = d_normed + nt(dqkv_s[rows, C:2 * C], wk[...])
        d_normed = d_normed + nt(dqkv_s[rows, 2 * C:3 * C], wv[...])
        upper = mid_s[rows, :].astype(F32)
        rinv = lax.rsqrt(jnp.mean(upper * upper, -1, keepdims=True) + 1e-06)
        term = jnp.sum(d_normed * upper * rinv, 0, keepdims=True)
        if h == 0:
            gain_s[...] = term
        else:
            gain_s[...] = gain_s[...] + term
        scaled = gain[...] * d_normed
        mean = jnp.mean(scaled * upper, -1, keepdims=True)
        d_mid = up_s[rows, :].astype(F32) + rinv * scaled - upper * (rinv * rinv * rinv) * mean
        d_mid = d_mid.astype(BF)
        wide = d_mid.astype(F32)
        frame = row_of((512, C)) % F
        dm_s[rows, 0:C] = jnp.where(frame == F - 1, 0.0, pltpu.roll(wide, 511, 0)).astype(BF)
        dm_s[rows, C:2 * C] = d_mid
        dm_s[rows, 2 * C:3 * C] = jnp.where(frame == 0, 0.0, pltpu.roll(wide, 1, 0)).astype(BF)
        back = nt(dm_s[rows, 0:C], wc[0])
        back = back + nt(dm_s[rows, C:2 * C], wc[1])
        back = back + nt(dm_s[rows, 2 * C:3 * C], wc[2])
        grad = wide + back
        for p in range(4):
            for i in range(4):
                t32[i, pl.ds(p, F, stride=4), :] = (
                    grad[p * F:(p + 1) * F, i * 128:i * 128 + 128])
        for i in range(4):
            osend[h, :, :, i * 128:i * 128 + 128] = t32[i].astype(BF).reshape(TM, 16, 128)

    sib = device(zl, 1 - c, x, y, zh)

    for h in range(2):
        arrived(ru, h, 2 + h)
        backward_att(h)

        @pl.loop(4 * h, 4 * h + 4)
        def _(p):
            backward_attend(p)

        grads_first(h)
        if h == 1:
            for i in range(4):
                g0s_a[:, i] = g_s[3 + i, :, 1 - c].astype(BF)
            send(g0s_a, g0r_a, ssem.at[6], rsem.at[6], sib)
        backward_dense(h)
        scatter(osend, orecv, h, 4 + h)
        grads_taps(h)

    for i in range(3):
        g0s_b[:, i] = g_s[i, :, 1 - c].astype(BF)
    send(g0s_b, g0r_b, ssem.at[7], rsem.at[7], sib)

    gn_s[...] = jnp.concatenate(
        [gain_s[:, i * 128:(i + 1) * 128] for i in range(4)] + [jnp.zeros((4, 128), F32)], 0)
    send(gn_s, gn0, ssem.at[8], rsem.at[8], sib)

    wait_bytes(g0r_a, rsem.at[6])
    for xx in range(4):
        for i in range(4):
            s1_a[xx, :, i] = (
                g_s[3 + i, xx * 4:xx * 4 + 4, c] + g0r_a[xx * 4:xx * 4 + 4, i].astype(F32)
            ).astype(BF)

    @pl.loop(1, 4)
    def _(k):
        to = (x + k) % 4
        send(s1_a.at[to], r1_a.at[x], ssem.at[9], rsem.at[9], device(zl, c, to, y, zh))

    wait_bytes(g0r_b, rsem.at[7])
    for xx in range(4):
        for i in range(3):
            s1_b[:, xx, i] = (
                g_s[i, xx * 4:xx * 4 + 4, c] + g0r_b[xx * 4:xx * 4 + 4, i].astype(F32)
            ).astype(BF)

    @pl.loop(1, 4)
    def _(k):
        to = (y + k) % 4
        send(s1_b.at[to], r1_b.at[y], ssem.at[10], rsem.at[10], device(zl, c, x, to, zh))

    wait_bytes(gn0, rsem.at[8])
    gnx[x] = gn_s[...] + gn0[...]

    @pl.loop(1, 4)
    def _(k):
        to = (x + k) % 4
        send(gnx.at[x], gnx.at[x], ssem.at[11], rsem.at[11], device(zl, c, to, y, zh))

    def total(ref, own, mine):
        acc = own[mine].astype(F32)
        for k in range(1, 4):
            acc = acc + ref[(mine + k) % 4].astype(F32)
        return acc

    wait_bytes(r1_a.at[pl.ds(0, 3)], rsem.at[9])
    s2_a[...] = total(r1_a, s1_a, x).astype(BF)

    @pl.loop(1, 4)
    def _(k):
        to = (y + k) % 4
        send(s2_a.at[to], r2_a.at[y], ssem.at[12], rsem.at[12], device(zl, c, x, to, zh))

    wait_bytes(r1_b.at[pl.ds(0, 3)], rsem.at[10])
    s2_b[...] = total(r1_b, s1_b, y).astype(BF)

    @pl.loop(1, 4)
    def _(k):
        to = (x + k) % 4
        send(s2_b.at[to], r2_b.at[x], ssem.at[13], rsem.at[13], device(zl, c, to, y, zh))

    wait_bytes(gnx.at[pl.ds(0, 3)], rsem.at[11])
    gny[y] = gnx[0] + gnx[1] + gnx[2] + gnx[3]

    @pl.loop(1, 4)
    def _(k):
        to = (y + k) % 4
        send(gny.at[y], gny.at[y], ssem.at[14], rsem.at[14], device(zl, c, x, to, zh))

    wait_bytes(r2_a.at[pl.ds(0, 3)], rsem.at[12])
    ta = total(r2_a, s2_a, y)
    wait_bytes(r2_b.at[pl.ds(0, 3)], rsem.at[13])
    tb = total(r2_b, s2_b, x)
    for q in range(4):
        t_s[q, 0:3] = tb[:, :, q * 128:q * 128 + 128]
        t_s[q, 3:7] = ta[:, :, q * 128:q * 128 + 128]

    wait_bytes(gny.at[pl.ds(0, 3)], rsem.at[14])
    gnz[z] = gny[0] + gny[1] + gny[2] + gny[3]

    @pl.loop(1, 8)
    def _(k):
        send(gnz.at[z], gnz.at[z], ssem.at[15], rsem.at[15], at_z((z + k) % 8, c))

    owner = c == zh

    @pl.loop(0, 4)
    def _(k):
        q = (zl + k) % 4

        @pl.when(jnp.logical_not(jnp.logical_and(owner, k == 0)))
        def _():
            send(t_s.at[q], zr.at[z], ssem.at[16], rsem.at[16], at_z(c * 4 + q, c))

    @pl.when(owner)
    def _():
        zr[z] = t_s[zl]
        wait_bytes(zr.at[pl.ds(0, 7)], rsem.at[16])
        acc = zr[0]
        for k in range(1, 8):
            acc = acc + zr[k]
        agr[zl] = acc

        @pl.loop(1, 8)
        def _(k):
            to = (zl * 2 + c + k) % 8
            send(agr.at[zl], agr.at[zl], ssem.at[17], rsem.at[17],
                 at_z(zh * 4 + to // 2, to % 2))

        wait_bytes(agr.at[pl.ds(0, 3)], rsem.at[17])

    @pl.when(jnp.logical_not(owner))
    def _():
        wait_bytes(agr, rsem.at[17])

    for q in range(4):
        ograds[:, :, q * 128:q * 128 + 128] = agr[q]

    wait_bytes(gnz.at[pl.ds(0, 7)], rsem.at[15])
    acc = gnz[0]
    for k in range(1, 8):
        acc = acc + gnz[k]
    ogain[...] = acc

    low = row_of((F, C)) % 8 < 4
    for h in range(2):
        arrived(orecv, h, 4 + h)
        got = [[], [], [], []]
        for m in range(16):
            for o in range(2):
                tile = orecv[h, 2 * m + o].astype(F32)
                got[o].append(tile[0:8])
                got[2 + o].append(tile[8:16])
        got = [jnp.concatenate(g, 0) for g in got]
        for f in (0, 2):
            even, odd = got[f], got[f + 1]
            out[f, 128 * h:128 * h + 128, :] = jnp.where(
                low, even, pltpu.roll(odd, 4, 0)).astype(BF)
            out[f + 1, 128 * h:128 * h + 128, :] = jnp.where(
                low, pltpu.roll(even, F - 4, 0), odd).astype(BF)

    for i, ref in enumerate((sbl, sbl, sbu, sbu, osend, osend)):
        wait_bytes(ref.at[i % 2, pl.ds(0, TM - 1)], ssem.at[i])
    wait_bytes(g0s_a, ssem.at[6])
    wait_bytes(g0s_b, ssem.at[7])
    wait_bytes(gn_s, ssem.at[8])
    wait_bytes(s1_a.at[pl.ds(0, 3)], ssem.at[9])
    wait_bytes(s1_b.at[pl.ds(0, 3)], ssem.at[10])
    wait_bytes(gnx.at[pl.ds(0, 3)], ssem.at[11])
    wait_bytes(s2_a.at[pl.ds(0, 3)], ssem.at[12])
    wait_bytes(s2_b.at[pl.ds(0, 3)], ssem.at[13])
    wait_bytes(gny.at[pl.ds(0, 3)], ssem.at[14])
    wait_bytes(gnz.at[pl.ds(0, 7)], ssem.at[15])

    @pl.when(owner)
    def _():
        wait_bytes(t_s.at[pl.ds(0, 3)], ssem.at[16])
        wait_bytes(zr.at[pl.ds(0, 7)], ssem.at[17])

    @pl.when(jnp.logical_not(owner))
    def _():
        wait_bytes(t_s, ssem.at[16])


def block(latents, upstream, conv_weight, w_query, w_key, w_value, w_out, norm_gain):
    v = lambda shape, dtype=BF: pltpu.VMEM(shape, dtype)
    scratch = [
        v((2, TM, 16, C)), v((2, TM, 16, C)), v((2, TM, 16, C)), v((2, TM, 16, C)),
        v((2, TM, 16, C)), v((2, TM, 16, C)),
        v((4, 512, 128), F32), v((1024, C)), v((1024, C)), v((1024, C)), v((1024, 3 * C)),
        v((32, 256, F), F32), v((1024, C)), v((1024, C)), v((1024, C)),
        v((1024, 3 * C)), v((1024, 3 * C)),
        v((7, 16, 2, 16, C), F32), v((1, C), F32),
        v((16, 4, 16, C)), v((16, 3, 16, C)), v((16, 4, 16, C)), v((16, 3, 16, C)),
        v((4, 4, 4, 16, C)), v((4, 4, 4, 16, C)), v((4, 4, 16, C)), v((4, 4, 16, C)),
        v((4, 4, 3, 16, C)), v((4, 4, 3, 16, C)), v((4, 3, 16, C)), v((4, 3, 16, C)),
        v((4, 7, 16, 128), F32), v((8, 7, 16, 128), F32), v((7, 16, 128), F32),
        v((4, 7, 16, 128), F32),
        v((8, 128), F32), v((8, 128), F32), v((4, 8, 128), F32), v((4, 8, 128), F32),
        v((8, 8, 128), F32),
        pltpu.SemaphoreType.DMA((18,)), pltpu.SemaphoreType.DMA((18,)),
    ]
    vmem = pl.BlockSpec(memory_space=pltpu.VMEM)
    return pl.pallas_call(
        kernel,
        out_shape=(
            jax.ShapeDtypeStruct((4, 256, C), BF),
            jax.ShapeDtypeStruct((7, 16, C), F32),
            jax.ShapeDtypeStruct((8, 128), F32),
        ),
        in_specs=[vmem] * 8,
        out_specs=(vmem, vmem, vmem),
        scratch_shapes=scratch,
        compiler_params=pltpu.CompilerParams(
            collective_id=0, has_side_effects=True, vmem_limit_bytes=60 * 2**20
        ),
        name="block_backward",
    )(latents, upstream, conv_weight, w_query, w_key, w_value, w_out, norm_gain)


def per_device(latents, upstream, conv_weight, w_query, w_key, w_value, w_out, norm_gain):
    grad_in, rows, gain_rows = block(
        latents[0], upstream[0], conv_weight, w_query, w_key, w_value, w_out, norm_gain[None]
    )
    gain_rows = lax.dynamic_slice(
        gain_rows.reshape(-1), (lax.axis_index("tm") * 16,), (16,))
    return (grad_in[None], rows[0:3], rows[3], rows[4], rows[5], rows[6], gain_rows)


def solution(mesh):
    return jax.shard_map(
        per_device,
        mesh=mesh,
        in_specs=(P("dp", "tm", None, None), P("dp", "tm", None, None),
                  P(), P(), P(), P(), P(), P()),
        out_specs=(
            P("dp", "tm", None, None),
            P(None, "tm", None),
            P("tm", None),
            P("tm", None),
            P("tm", None),
            P("tm", None),
            P("tm"),
        ),
        check_vma=False,
    )
```

time: 697 us -> 128 us (0.18)
  waiting for transfers between devices: 293 us -> 0 us
  blocking collectives: 161 us -> 0 us
  Pallas kernels: 0 us -> 120 us
  local copies, waits for them, and re-layouts: 87.1 us -> 6.53 us
  matrix products: 71.9 us -> 0 us
  starting transfers between devices: 59.9 us -> 0 us
  between operations: 15.3 us -> 0.65 us
    reduce_scatter x1 -> x0, waiting for transfers between devices: 163 us -> none  [per_device(): lax.psum_scatter(terms, 'tm', scatter_dimension=1, tiled=True)]
    pallas_call x0 -> x1, Pallas kernels: none -> 120 us  [block(): pl.pallas_call(kernel, out_shape=(jax.ShapeDtypeStruct((4, 256, C), BF),...]
    unnamed x1 -> x0, blocking collectives: 119 us -> none
    dot_general x21 -> x0, matrix products: 66.8 us -> none  [the longest x5 13.9 us: cross(): lax.dot_general(left, right, (((0,), (0,)), ((), ())), preferred_element_...]
    psum x1 -> x0, waiting for transfers between devices: 66.8 us -> none  [per_device(): rows, gain_rows = lax.psum((rows, gain_rows), 'dp')]
    ppermute x4 -> x0, waiting for transfers between devices: 56.9 us -> none  [the longest x2 34.6 us: padded_2(): lax.ppermute(head, axis, [((i + 1) % count, i) for i in range(ends)])]
    reshape x13 -> x0, local copies, waits for them, and re-layouts: 48.1 us -> none  [the longest x2 8.05 us: attend_back(): k4 = keyed.reshape(shape4)]
    all_to_all x3 -> x0, starting transfers between devices: 47.9 us -> none  [the longest x1 26.4 us: per_device(): lax.all_to_all(mid, 'tm', split_axis=2, concat_axis=1, tiled=True)]
  transfers between devices with their start and end apart: 9 -> 0, of which waited for: 7 -> 0; matrix products, arithmetic and copies ran while one was open for 6% -> 0% of each run, Pallas kernels for 0% -> 0%
where the time goes in v1:
time: 128 us
  Pallas kernels  120 us (94%)
  local copies, waits for them, and re-layouts  6.53 us (5%)
    pallas_call x1, Pallas kernels, block(): pl.pallas_call(kernel, out_shape=(jax.ShapeDtypeStruct((4, 256, C), BF),...  120 us

profile of v1, /device:TPU:1, one launch (start us, length us, event | category | flops | bytes accessed | tf_op | source)
XLA Modules:
  0.0 127.7 jit_solution(2249234797889924287)
XLA Ops:
  0.6 120.5 %block_backward.1 = (bf16[4,256,512]{2,1,0:T(8,128)(2,1)}, f32[7,16,512]{2,1,0:T(8,128)}, f32[8,128]{1,0:T(8,128)}) custom-call(bf16[4,256,512]{2,1,0:T(8,128)(2,1)} %bitcast.14, bf16[4,256,512]{2,1,0:T(8,128)(2,1)} %bitcast.15, bf16[3,512,512]{2,1,0:T(8,128)(2,1)} %wc.1, bf16[512,512]{1,0:T(8,128)(2,1)} %wq.1, bf16[512,512]{1,0:T(8,128)(2,1)} %wk.1, ...), custom_call_target="tpu_custom_call" | custom-call | tf_op jit(solution)/shard_map/block_backward/pallas_call | solution.py:464
  121.1 1.3 dynamic_slice.3
  122.4 1.5 %slice_bitcast_fusion = (f32[16,512]{1,0:T(8,128)}, f32[16,512]{1,0:T(8,128)}, f32[16,512]{1,0:T(8,128)}, f32[16,512]{1,0:T(8,128)}) fusion(f32[7,16,512]{2,1,0:T(8,128)} %get-tuple-element.11), kind=kLoop, calls=%fused_computation | loop fusion | bytes 262144 | tf_op jit(solution)/shard_map/squeeze | solution.py:487
  123.9 1.5 %slice.15 = f32[3,16,512]{2,1,0:T(8,128)} slice(f32[7,16,512]{2,1,0:T(8,128)} %get-tuple-element.11), slice={[0:3], [0:16], [0:512]} | slice | bytes 196608 | tf_op jit(solution)/shard_map/slice | solution.py:487
  125.4 2.3 %copy.16 = bf16[1,4,256,512]{3,2,1,0:T(8,128)(2,1)} copy(bf16[1,4,256,512]{3,2,1,0:T(8,128)(2,1)} %bitcast.13) | data formatting | bytes 2097152

commit v2 on v1

--- a/solution.py
+++ b/solution.py
@@ -64,16 +64,30 @@
     return jnp.where(lane < 64, a[:F], a[F:])
 
 
+GROUPS = ((6,), (3, 4, 5), (0, 1, 2))
+
+
 def kernel(
-    lat, up, wc, wq, wk, wv, wo, gain,
-    out, ograds, ogain,
-    sbl, sbu, rl, ru, osend, orecv,
+    lat_in, up_in, wc_in, wq_in, wk_in, wv_in, wo_in, gain,
+    orecv, og0, og1, og2, ogain,
+    lat, up, wc, wq, wk, wv, wo,
+    sbl, sbu, rl, ru, osend,
     t32, x_s, mid_s, nrm_s, qkv_s, pr_s, att_s, up_s, da_s, dqkv_s, dm_s,
-    g_s, gain_s, g0s_a, g0s_b, g0r_a, g0r_b,
-    s1_a, r1_a, s2_a, r2_a, s1_b, r1_b, s2_b, r2_b,
-    t_s, zr, zsum, agr, gn_s, gn0, gnx, gny, gnz,
-    ssem, rsem,
+    g_s, gain_s, gn_s, gn0, gnx, gny, gnz,
+    *rest,
 ):
+    ssem, rsem, lsem = rest[-3:]
+    red = [dict(zip(("g0s", "g0r", "s1x", "r1x", "s1y", "r1y", "s2x", "r2x", "s2y", "r2y",
+                     "ts", "zr"), rest[12 * i:12 * i + 12])) for i in range(3)]
+    agr = (og0, og1, og2)
+    loads = [
+        pltpu.make_async_copy(src, dst, lsem.at[i])
+        for i, (src, dst) in enumerate(
+            ((lat_in, lat), (up_in, up), (wc_in, wc), (wq_in, wq), (wk_in, wk),
+             (wv_in, wv), (wo_in, wo)))
+    ]
+    for load in loads:
+        load.start()
     w = where_am_i()
     me, c, x, y, zl, zh = w["tm"], w["c"], w["x"], w["y"], w["zl"], w["zh"]
     z = zh * 4 + zl
@@ -119,18 +133,25 @@
             to = (me + k) % TM
             send(src.at[h, to], dst.at[h, me], ssem.at[i], rsem.at[i],
                  {"dp": w["dp"], "tm": to})
-        dst[h, me] = src[h, me]
 
     def arrived(dst, h, i):
         wait_bytes(dst.at[h, pl.ds(0, TM - 1)], rsem.at[i])
 
+    loads[0].wait()
     regroup(lat, sbl, 0)
     regroup(lat, sbl, 1)
     pl.semaphore_wait(barrier, 41)
     scatter(sbl, rl, 0, 0)
     scatter(sbl, rl, 1, 1)
+    for h in range(2):
+        rl[h, me] = sbl[h, me]
+    loads[1].wait()
     regroup(up, sbu, 0)
     regroup(up, sbu, 1)
+    for h in range(2):
+        ru[h, me] = sbu[h, me]
+    for load in loads[2:]:
+        load.wait()
 
     def by_pixel(src, dst, h):
         wide = src[h].reshape(512, C).astype(F32)
@@ -214,9 +235,12 @@
         else:
             g_s[i] = g_s[i] + value
 
+    def grads_out(h):
+        rows = pl.ds(h * 512, 512)
+        put(6, h, tn(att_s[rows, :], up_s[rows, :]))
+
     def grads_first(h):
         rows = pl.ds(h * 512, 512)
-        put(6, h, tn(att_s[rows, :], up_s[rows, :]))
         for i in range(3):
             put(3 + i, h, tn(nrm_s[rows, :], dqkv_s[rows, i * C:(i + 1) * C]))
 
@@ -259,63 +283,36 @@
             osend[h, :, :, i * 128:i * 128 + 128] = t32[i].astype(BF).reshape(TM, 16, 128)
 
     sib = device(zl, 1 - c, x, y, zh)
-
-    for h in range(2):
-        arrived(ru, h, 2 + h)
-        backward_att(h)
-
-        @pl.loop(4 * h, 4 * h + 4)
-        def _(p):
-            backward_attend(p)
-
-        grads_first(h)
-        if h == 1:
-            for i in range(4):
-                g0s_a[:, i] = g_s[3 + i, :, 1 - c].astype(BF)
-            send(g0s_a, g0r_a, ssem.at[6], rsem.at[6], sib)
-        backward_dense(h)
-        scatter(osend, orecv, h, 4 + h)
-        grads_taps(h)
-
-    for i in range(3):
-        g0s_b[:, i] = g_s[i, :, 1 - c].astype(BF)
-    send(g0s_b, g0r_b, ssem.at[7], rsem.at[7], sib)
-
-    gn_s[...] = jnp.concatenate(
-        [gain_s[:, i * 128:(i + 1) * 128] for i in range(4)] + [jnp.zeros((4, 128), F32)], 0)
-    send(gn_s, gn0, ssem.at[8], rsem.at[8], sib)
-
-    wait_bytes(g0r_a, rsem.at[6])
-    for xx in range(4):
-        for i in range(4):
-            s1_a[xx, :, i] = (
-                g_s[3 + i, xx * 4:xx * 4 + 4, c] + g0r_a[xx * 4:xx * 4 + 4, i].astype(F32)
-            ).astype(BF)
-
-    @pl.loop(1, 4)
-    def _(k):
-        to = (x + k) % 4
-        send(s1_a.at[to], r1_a.at[x], ssem.at[9], rsem.at[9], device(zl, c, to, y, zh))
-
-    wait_bytes(g0r_b, rsem.at[7])
-    for xx in range(4):
-        for i in range(3):
-            s1_b[:, xx, i] = (
-                g_s[i, xx * 4:xx * 4 + 4, c] + g0r_b[xx * 4:xx * 4 + 4, i].astype(F32)
-            ).astype(BF)
-
-    @pl.loop(1, 4)
-    def _(k):
-        to = (y + k) % 4
-        send(s1_b.at[to], r1_b.at[y], ssem.at[10], rsem.at[10], device(zl, c, x, to, zh))
-
-    wait_bytes(gn0, rsem.at[8])
-    gnx[x] = gn_s[...] + gn0[...]
-
-    @pl.loop(1, 4)
-    def _(k):
-        to = (x + k) % 4
-        send(gnx.at[x], gnx.at[x], ssem.at[11], rsem.at[11], device(zl, c, to, y, zh))
+    owner = c == zh
+    not_owner = jnp.logical_not(owner)
+
+    def to_x(to):
+        return device(zl, c, to, y, zh)
+
+    def to_y(to):
+        return device(zl, c, x, to, zh)
+
+    def red_cores(g):
+        r = red[g]
+        for i, m in enumerate(GROUPS[g]):
+            r["g0s"][:, i] = g_s[m, :, 1 - c].astype(BF)
+        send(r["g0s"], r["g0r"], ssem.at[6 + 7 * g], rsem.at[6 + 7 * g], sib)
+
+    def red_first(g):
+        r, s = red[g], 7 + 7 * g
+        wait_bytes(r["g0r"], rsem.at[6 + 7 * g])
+        for i, m in enumerate(GROUPS[g]):
+            for xx in range(4):
+                four = slice(xx * 4, xx * 4 + 4)
+                both = g_s[m, four, c] + r["g0r"][four, i].astype(F32)
+                r["s1x"][xx, :, i] = both[:, :, :256].astype(BF)
+                r["s1y"][:, xx, i] = both[:, :, 256:].astype(BF)
+
+        @pl.loop(1, 4)
+        def _(k):
+            tx, ty = (x + k) % 4, (y + k) % 4
+            send(r["s1x"].at[tx], r["r1x"].at[x], ssem.at[s], rsem.at[s], to_x(tx))
+            send(r["s1y"].at[ty], r["r1y"].at[y], ssem.at[s + 1], rsem.at[s + 1], to_y(ty))
 
     def total(ref, own, mine):
         acc = own[mine].astype(F32)
@@ -323,88 +320,190 @@
             acc = acc + ref[(mine + k) % 4].astype(F32)
         return acc
 
-    wait_bytes(r1_a.at[pl.ds(0, 3)], rsem.at[9])
-    s2_a[...] = total(r1_a, s1_a, x).astype(BF)
-
-    @pl.loop(1, 4)
-    def _(k):
-        to = (y + k) % 4
-        send(s2_a.at[to], r2_a.at[y], ssem.at[12], rsem.at[12], device(zl, c, x, to, zh))
-
-    wait_bytes(r1_b.at[pl.ds(0, 3)], rsem.at[10])
-    s2_b[...] = total(r1_b, s1_b, y).astype(BF)
-
-    @pl.loop(1, 4)
-    def _(k):
-        to = (x + k) % 4
-        send(s2_b.at[to], r2_b.at[x], ssem.at[13], rsem.at[13], device(zl, c, to, y, zh))
-
-    wait_bytes(gnx.at[pl.ds(0, 3)], rsem.at[11])
-    gny[y] = gnx[0] + gnx[1] + gnx[2] + gnx[3]
-
-    @pl.loop(1, 4)
-    def _(k):
-        to = (y + k) % 4
-        send(gny.at[y], gny.at[y], ssem.at[14], rsem.at[14], device(zl, c, x, to, zh))
-
-    wait_bytes(r2_a.at[pl.ds(0, 3)], rsem.at[12])
-    ta = total(r2_a, s2_a, y)
-    wait_bytes(r2_b.at[pl.ds(0, 3)], rsem.at[13])
-    tb = total(r2_b, s2_b, x)
-    for q in range(4):
-        t_s[q, 0:3] = tb[:, :, q * 128:q * 128 + 128]
-        t_s[q, 3:7] = ta[:, :, q * 128:q * 128 + 128]
-
-    wait_bytes(gny.at[pl.ds(0, 3)], rsem.at[14])
-    gnz[z] = gny[0] + gny[1] + gny[2] + gny[3]
-
-    @pl.loop(1, 8)
-    def _(k):
-        send(gnz.at[z], gnz.at[z], ssem.at[15], rsem.at[15], at_z((z + k) % 8, c))
-
-    owner = c == zh
+    def red_second(g):
+        r, s = red[g], 7 + 7 * g
+        wait_bytes(r["r1x"].at[pl.ds(0, 3)], rsem.at[s])
+        r["s2x"][...] = total(r["r1x"], r["s1x"], x).astype(BF)
+
+        @pl.loop(1, 4)
+        def _(k):
+            ty = (y + k) % 4
+            send(r["s2x"].at[ty], r["r2x"].at[y], ssem.at[s + 2], rsem.at[s + 2], to_y(ty))
+
+        wait_bytes(r["r1y"].at[pl.ds(0, 3)], rsem.at[s + 1])
+        r["s2y"][...] = total(r["r1y"], r["s1y"], y).astype(BF)
+
+        @pl.loop(1, 4)
+        def _(k):
+            tx = (x + k) % 4
+            send(r["s2y"].at[tx], r["r2y"].at[x], ssem.at[s + 3], rsem.at[s + 3], to_x(tx))
+
+    def red_z(g):
+        r, s = red[g], 7 + 7 * g
+        wait_bytes(r["r2x"].at[pl.ds(0, 3)], rsem.at[s + 2])
+        half = total(r["r2x"], r["s2x"], y).astype(BF)
+        r["ts"][0] = half[:, :, :128]
+        r["ts"][1] = half[:, :, 128:]
+        wait_bytes(r["r2y"].at[pl.ds(0, 3)], rsem.at[s + 3])
+        half = total(r["r2y"], r["s2y"], x).astype(BF)
+        r["ts"][2] = half[:, :, :128]
+        r["ts"][3] = half[:, :, 128:]
+
+        @pl.loop(0, 4)
+        def _(k):
+            q = (zl + k) % 4
+
+            @pl.when(jnp.logical_or(not_owner, k != 0))
+            def _():
+                send(r["ts"].at[q], r["zr"].at[z], ssem.at[s + 4], rsem.at[s + 4],
+                     at_z(c * 4 + q, c))
+
+    def red_gather(g):
+        r, s = red[g], 7 + 7 * g
+
+        @pl.when(owner)
+        def _():
+            r["zr"][z] = r["ts"][zl]
+            wait_bytes(r["zr"].at[pl.ds(0, 7)], rsem.at[s + 4])
+            acc = r["zr"][0].astype(F32)
+            for k in range(1, 8):
+                acc = acc + r["zr"][k].astype(F32)
+            agr[g][zl] = acc.astype(BF)
+
+            @pl.loop(1, 8)
+            def _(k):
+                to = (zl * 2 + c + k) % 8
+                send(agr[g].at[zl], agr[g].at[zl], ssem.at[s + 5], rsem.at[s + 5],
+                     at_z(zh * 4 + to // 2, to % 2))
+
+    def red_end(g):
+        r, s = red[g], 7 + 7 * g
+
+        @pl.when(owner)
+        def _():
+            wait_bytes(agr[g].at[pl.ds(0, 3)], rsem.at[s + 5])
+            wait_bytes(r["ts"].at[pl.ds(0, 3)], ssem.at[s + 4])
+            wait_bytes(r["zr"].at[pl.ds(0, 7)], ssem.at[s + 5])
+
+        @pl.when(not_owner)
+        def _():
+            wait_bytes(agr[g], rsem.at[s + 5])
+            wait_bytes(r["ts"], ssem.at[s + 4])
+
+        wait_bytes(r["g0s"], ssem.at[6 + 7 * g])
+        wait_bytes(r["s1x"].at[pl.ds(0, 3)], ssem.at[s])
+        wait_bytes(r["s1y"].at[pl.ds(0, 3)], ssem.at[s + 1])
+        wait_bytes(r["s2x"].at[pl.ds(0, 3)], ssem.at[s + 2])
+        wait_bytes(r["s2y"].at[pl.ds(0, 3)], ssem.at[s + 3])
+
+    def gain_cores():
+        gn_s[...] = jnp.concatenate(
+            [gain_s[:, i * 128:(i + 1) * 128] for i in range(4)] + [jnp.zeros((4, 128), F32)], 0)
+        send(gn_s, gn0, ssem.at[27], rsem.at[27], sib)
+
+    def gain_x():
+        wait_bytes(gn0, rsem.at[27])
+        gnx[x] = gn_s[...] + gn0[...]
+
+        @pl.loop(1, 4)
+        def _(k):
+            send(gnx.at[x], gnx.at[x], ssem.at[28], rsem.at[28], to_x((x + k) % 4))
+
+    def gain_y():
+        wait_bytes(gnx.at[pl.ds(0, 3)], rsem.at[28])
+        gny[y] = gnx[0] + gnx[1] + gnx[2] + gnx[3]
+
+        @pl.loop(1, 4)
+        def _(k):
+            send(gny.at[y], gny.at[y], ssem.at[29], rsem.at[29], to_y((y + k) % 4))
+
+    def gain_z():
+        wait_bytes(gny.at[pl.ds(0, 3)], rsem.at[29])
+        gnz[z] = gny[0] + gny[1] + gny[2] + gny[3]
+
+        @pl.loop(1, 8)
+        def _(k):
+            send(gnz.at[z], gnz.at[z], ssem.at[30], rsem.at[30], at_z((z + k) % 8, c))
+
+    def gain_end():
+        wait_bytes(gnz.at[pl.ds(0, 7)], rsem.at[30])
+        acc = gnz[0]
+        for k in range(1, 8):
+            acc = acc + gnz[k]
+        ogain[...] = acc
+        wait_bytes(gn_s, ssem.at[27])
+        wait_bytes(gnx.at[pl.ds(0, 3)], ssem.at[28])
+        wait_bytes(gny.at[pl.ds(0, 3)], ssem.at[29])
+        wait_bytes(gnz.at[pl.ds(0, 7)], ssem.at[30])
+
+    own_out = [pltpu.make_async_copy(osend.at[h, me], orecv.at[h, me], lsem.at[7 + h])
+               for h in range(2)]
+
+    arrived(ru, 0, 2)
+    backward_att(0)
 
     @pl.loop(0, 4)
-    def _(k):
-        q = (zl + k) % 4
-
-        @pl.when(jnp.logical_not(jnp.logical_and(owner, k == 0)))
-        def _():
-            send(t_s.at[q], zr.at[z], ssem.at[16], rsem.at[16], at_z(c * 4 + q, c))
-
-    @pl.when(owner)
-    def _():
-        zr[z] = t_s[zl]
-        wait_bytes(zr.at[pl.ds(0, 7)], rsem.at[16])
-        acc = zr[0]
-        for k in range(1, 8):
-            acc = acc + zr[k]
-        agr[zl] = acc
-
-        @pl.loop(1, 8)
-        def _(k):
-            to = (zl * 2 + c + k) % 8
-            send(agr.at[zl], agr.at[zl], ssem.at[17], rsem.at[17],
-                 at_z(zh * 4 + to // 2, to % 2))
-
-        wait_bytes(agr.at[pl.ds(0, 3)], rsem.at[17])
-
-    @pl.when(jnp.logical_not(owner))
-    def _():
-        wait_bytes(agr, rsem.at[17])
-
-    for q in range(4):
-        ograds[:, :, q * 128:q * 128 + 128] = agr[q]
-
-    wait_bytes(gnz.at[pl.ds(0, 7)], rsem.at[15])
-    acc = gnz[0]
-    for k in range(1, 8):
-        acc = acc + gnz[k]
-    ogain[...] = acc
-
+    def _(p):
+        backward_attend(p)
+
+    grads_out(0)
+    grads_first(0)
+    backward_dense(0)
+    grads_taps(0)
+    scatter(osend, orecv, 0, 4)
+    own_out[0].start()
+
+    arrived(ru, 1, 3)
+    backward_att(1)
+    grads_out(1)
+    red_cores(0)
+
+    @pl.loop(4, 6)
+    def _(p):
+        backward_attend(p)
+
+    red_first(0)
+
+    @pl.loop(6, 8)
+    def _(p):
+        backward_attend(p)
+
+    grads_first(1)
+    red_cores(1)
+    red_second(0)
+    backward_dense(1)
+    red_first(1)
+    gain_cores()
+    scatter(osend, orecv, 1, 5)
+    own_out[1].start()
+    grads_taps(1)
+    red_cores(2)
+    red_z(0)
+    gain_x()
+    red_first(2)
+    red_gather(0)
+    red_second(1)
+    gain_y()
+    red_second(2)
+    red_z(1)
+    gain_z()
+    red_z(2)
+    red_gather(1)
+    red_gather(2)
+    for g in range(3):
+        red_end(g)
+    gain_end()
+
+    for h in range(2):
+        arrived(orecv, h, 4 + h)
+        own_out[h].wait()
+    for i, ref in enumerate((sbl, sbl, sbu, sbu, osend, osend)):
+        wait_bytes(ref.at[i % 2, pl.ds(0, TM - 1)], ssem.at[i])
+
+
+def finish(orecv, og0, og1, og2, ogain, out, conv, query, key, value, outer, gain):
     low = row_of((F, C)) % 8 < 4
     for h in range(2):
-        arrived(orecv, h, 4 + h)
         got = [[], [], [], []]
         for m in range(16):
             for o in range(2):
@@ -418,73 +517,75 @@
                 low, even, pltpu.roll(odd, 4, 0)).astype(BF)
             out[f + 1, 128 * h:128 * h + 128, :] = jnp.where(
                 low, pltpu.roll(even, F - 4, 0), odd).astype(BF)
-
-    for i, ref in enumerate((sbl, sbl, sbu, sbu, osend, osend)):
-        wait_bytes(ref.at[i % 2, pl.ds(0, TM - 1)], ssem.at[i])
-    wait_bytes(g0s_a, ssem.at[6])
-    wait_bytes(g0s_b, ssem.at[7])
-    wait_bytes(gn_s, ssem.at[8])
-    wait_bytes(s1_a.at[pl.ds(0, 3)], ssem.at[9])
-    wait_bytes(s1_b.at[pl.ds(0, 3)], ssem.at[10])
-    wait_bytes(gnx.at[pl.ds(0, 3)], ssem.at[11])
-    wait_bytes(s2_a.at[pl.ds(0, 3)], ssem.at[12])
-    wait_bytes(s2_b.at[pl.ds(0, 3)], ssem.at[13])
-    wait_bytes(gny.at[pl.ds(0, 3)], ssem.at[14])
-    wait_bytes(gnz.at[pl.ds(0, 7)], ssem.at[15])
-
-    @pl.when(owner)
-    def _():
-        wait_bytes(t_s.at[pl.ds(0, 3)], ssem.at[16])
-        wait_bytes(zr.at[pl.ds(0, 7)], ssem.at[17])
-
-    @pl.when(jnp.logical_not(owner))
-    def _():
-        wait_bytes(t_s, ssem.at[16])
+    for q in range(4):
+        lanes = slice(q * 128, q * 128 + 128)
+        outer[:, lanes] = og0[q, 0].astype(F32)
+        for i, ref in enumerate((query, key, value)):
+            ref[:, lanes] = og1[q, i].astype(F32)
+        conv[:, :, lanes] = og2[q].astype(F32)
+    tm = lax.axis_index("tm")
+    row = ogain[pl.ds(tm // 8, 1), :]
+    gain[...] = pltpu.roll(row, (128 - (tm % 8) * 16) % 128, 1)[0, :16]
 
 
 def block(latents, upstream, conv_weight, w_query, w_key, w_value, w_out, norm_gain):
     v = lambda shape, dtype=BF: pltpu.VMEM(shape, dtype)
     scratch = [
+        v((4, 256, C)), v((4, 256, C)), v((3, C, C)), v((C, C)), v((C, C)), v((C, C)), v((C, C)),
         v((2, TM, 16, C)), v((2, TM, 16, C)), v((2, TM, 16, C)), v((2, TM, 16, C)),
-        v((2, TM, 16, C)), v((2, TM, 16, C)),
+        v((2, TM, 16, C)),
         v((4, 512, 128), F32), v((1024, C)), v((1024, C)), v((1024, C)), v((1024, 3 * C)),
         v((32, 256, F), F32), v((1024, C)), v((1024, C)), v((1024, C)),
         v((1024, 3 * C)), v((1024, 3 * C)),
         v((7, 16, 2, 16, C), F32), v((1, C), F32),
-        v((16, 4, 16, C)), v((16, 3, 16, C)), v((16, 4, 16, C)), v((16, 3, 16, C)),
-        v((4, 4, 4, 16, C)), v((4, 4, 4, 16, C)), v((4, 4, 16, C)), v((4, 4, 16, C)),
-        v((4, 4, 3, 16, C)), v((4, 4, 3, 16, C)), v((4, 3, 16, C)), v((4, 3, 16, C)),
-        v((4, 7, 16, 128), F32), v((8, 7, 16, 128), F32), v((7, 16, 128), F32),
-        v((4, 7, 16, 128), F32),
         v((8, 128), F32), v((8, 128), F32), v((4, 8, 128), F32), v((4, 8, 128), F32),
         v((8, 8, 128), F32),
-        pltpu.SemaphoreType.DMA((18,)), pltpu.SemaphoreType.DMA((18,)),
     ]
+    for group in GROUPS:
+        n = len(group)
+        scratch += [v((16, n, 16, C))] * 2 + [v((4, 4, n, 16, 256))] * 4
+        scratch += [v((4, n, 16, 256))] * 4 + [v((4, n, 16, 128)), v((8, n, 16, 128))]
+    scratch += [pltpu.SemaphoreType.DMA((31,)), pltpu.SemaphoreType.DMA((31,)),
+                pltpu.SemaphoreType.DMA((9,))]
     vmem = pl.BlockSpec(memory_space=pltpu.VMEM)
-    return pl.pallas_call(
+    hbm = pl.BlockSpec(memory_space=pl.ANY)
+    got = pl.pallas_call(
         kernel,
         out_shape=(
-            jax.ShapeDtypeStruct((4, 256, C), BF),
-            jax.ShapeDtypeStruct((7, 16, C), F32),
+            jax.ShapeDtypeStruct((2, TM, 16, C), BF),
+            jax.ShapeDtypeStruct((4, 1, 16, 128), BF),
+            jax.ShapeDtypeStruct((4, 3, 16, 128), BF),
+            jax.ShapeDtypeStruct((4, 3, 16, 128), BF),
             jax.ShapeDtypeStruct((8, 128), F32),
         ),
-        in_specs=[vmem] * 8,
-        out_specs=(vmem, vmem, vmem),
+        in_specs=[hbm] * 7 + [vmem],
+        out_specs=(hbm, vmem, vmem, vmem, vmem),
         scratch_shapes=scratch,
         compiler_params=pltpu.CompilerParams(
             collective_id=0, has_side_effects=True, vmem_limit_bytes=60 * 2**20
         ),
         name="block_backward",
     )(latents, upstream, conv_weight, w_query, w_key, w_value, w_out, norm_gain)
+    rows = jax.ShapeDtypeStruct((16, C), F32)
+    return pl.pallas_call(
+        finish,
+        out_shape=(
+            jax.ShapeDtypeStruct((4, 256, C), BF),
+            jax.ShapeDtypeStruct((3, 16, C), F32),
+            rows, rows, rows, rows,
+            jax.ShapeDtypeStruct((16,), F32),
+        ),
+        in_specs=[vmem] * 5,
+        out_specs=(vmem,) * 7,
+        name="finish",
+    )(*got)
 
 
 def per_device(latents, upstream, conv_weight, w_query, w_key, w_value, w_out, norm_gain):
-    grad_in, rows, gain_rows = block(
+    grad_in, *grads = block(
         latents[0], upstream[0], conv_weight, w_query, w_key, w_value, w_out, norm_gain[None]
     )
-    gain_rows = lax.dynamic_slice(
-        gain_rows.reshape(-1), (lax.axis_index("tm") * 16,), (16,))
-    return (grad_in[None], rows[0:3], rows[3], rows[4], rows[5], rows[6], gain_rows)
+    return (grad_in[None], *grads)
 
 
 def solution(mesh):

time: 128 us -> 115 us (0.90)
  local copies, waits for them, and re-layouts: 6.53 us -> 0 us
  Pallas kernels: 120 us -> 114 us
    pallas_call x1 -> x2, Pallas kernels: 120 us -> 114 us  [the longest x1 111 us: block(): pl.pallas_call(kernel, out_shape=(jax.ShapeDtypeStruct((2, TM, 16, C), BF...]
    unnamed x1 -> x0, local copies, waits for them, and re-layouts: 2.26 us -> none
    slice x1 -> x0, local copies, waits for them, and re-layouts: 1.54 us -> none  [per_device(): rows[0:3]]
    squeeze x1 -> x0, local copies, waits for them, and re-layouts: 1.46 us -> none  [per_device(): rows[6]]
where the time goes in v2:
time: 115 us
  Pallas kernels  114 us (99%)
    pallas_call x1, Pallas kernels, block(): pl.pallas_call(kernel, out_shape=(jax.ShapeDtypeStruct((2, TM, 16, C), BF...  111 us
    pallas_call x1, Pallas kernels, block(): pl.pallas_call(finish, out_shape=(jax.ShapeDtypeStruct((4, 256, C), BF),...  2.94 us

profile of v2, /device:TPU:1, one launch (start us, length us, event | category | flops | bytes accessed | tf_op | source)
XLA Modules:
  0.0 114.9 jit_solution(13638777280748485167)
XLA Ops:
  0.6 111.4 %block_backward.1 = (bf16[2,32,16,512]{3,2,1,0:T(8,128)(2,1)}, bf16[4,1,16,128]{3,2,1,0:T(8,128)(2,1)}, bf16[4,3,16,128]{3,2,1,0:T(8,128)(2,1)}, bf16[4,3,16,128]{3,2,1,0:T(8,128)(2,1)}, f32[8,128]{1,0:T(8,128)}) custom-call(bf16[4,256,512]{2,1,0:T(8,128)(2,1)} %bitcast.4, bf16[4,256,512]{2,1,0:T(8,128)(2,1)} %bitcast.5, bf16[3,512,512]{2,1,0:T(8,128)(2,1)} %wc_in.1, ...), custom_call_target="tpu_custom_call" | custom-call | tf_op jit(solution)/shard_map/block_backward/pallas_call | solution.py:552
  112.0 2.9 %finish.1 = (bf16[4,256,512]{2,1,0:T(8,128)(2,1)}, f32[3,16,512]{2,1,0:T(8,128)}, f32[16,512]{1,0:T(8,128)}, f32[16,512]{1,0:T(8,128)}, f32[16,512]{1,0:T(8,128)}, /*index=5*/f32[16,512]{1,0:T(8,128)}, f32[16]{0:T(128)}) custom-call(bf16[2,32,16,512]{3,2,1,0:T(8,128)(2,1)} %get-tuple-element.19.orecv, bf16[4,1,16,128]{3,2,1,0:T(8,128)(2,1)} %get-tuple-element.20.og0, ...), custom_call_target="tpu_custom_call" | custom-call | tf_op jit(solution)/shard_map/finish/pallas_call | solution.py:570

commit v3 on v2

--- a/solution.py
+++ b/solution.py
@@ -64,22 +64,24 @@
     return jnp.where(lane < 64, a[:F], a[F:])
 
 
-GROUPS = ((6,), (3, 4, 5), (0, 1, 2))
+GROUPS = ((6, 5), (3, 4), (0,), (1,), (2,))
+NG = len(GROUPS)
+GS = 6 + 7 * NG
 
 
 def kernel(
     lat_in, up_in, wc_in, wq_in, wk_in, wv_in, wo_in, gain,
-    orecv, og0, og1, og2, ogain,
+    orecv, og0, og1, og2, og3, og4, ogain,
     lat, up, wc, wq, wk, wv, wo,
     sbl, sbu, rl, ru, osend,
-    t32, x_s, mid_s, nrm_s, qkv_s, pr_s, att_s, up_s, da_s, dqkv_s, dm_s,
+    t32, x_s, mid_s, nt_s, xt_s, at_s, qkv_s, pr_s, up_s, da_s, dqkv_s, dm_s,
     g_s, gain_s, gn_s, gn0, gnx, gny, gnz,
     *rest,
 ):
     ssem, rsem, lsem = rest[-3:]
     red = [dict(zip(("g0s", "g0r", "s1x", "r1x", "s1y", "r1y", "s2x", "r2x", "s2y", "r2y",
-                     "ts", "zr"), rest[12 * i:12 * i + 12])) for i in range(3)]
-    agr = (og0, og1, og2)
+                     "ts", "zr"), rest[12 * i:12 * i + 12])) for i in range(NG)]
+    agr = (og0, og1, og2, og3, og4)
     loads = [
         pltpu.make_async_copy(src, dst, lsem.at[i])
         for i, (src, dst) in enumerate(
@@ -127,8 +129,8 @@
                     [tiles[0][o][m], tiles[1][o][m]], 0
                 ).astype(BF)
 
-    def scatter(src, dst, h, i):
-        @pl.loop(1, TM)
+    def scatter(src, dst, h, i, lo=1, hi=TM):
+        @pl.loop(lo, hi)
         def _(k):
             to = (me + k) % TM
             send(src.at[h, to], dst.at[h, me], ssem.at[i], rsem.at[i],
@@ -176,21 +178,25 @@
         upper = mid.astype(F32)
         rinv = lax.rsqrt(jnp.mean(upper * upper, -1, keepdims=True) + 1e-06)
         normed = (upper * rinv * gain[...]).astype(BF)
-        nrm_s[rows, :] = normed
+        nt_s[h] = normed.T
+        xt_s[h] = xx.T
         for i, weight in enumerate((wq, wk, wv)):
             qkv_s[rows, i * C:(i + 1) * C] = nn(normed, weight[...]).astype(BF)
 
     def forward_attend(p):
         rows = pl.ds(pl.multiple_of(p * F, F), F)
+        cols = pl.ds(pl.multiple_of(p % 4 * F, F), F)
+        scores = []
         for j in range(4):
             q = qkv_s[rows, j * 128:j * 128 + 128]
             k2 = split_heads(qkv_s[rows, C + j * 128:C + j * 128 + 128])
+            scores.append((nt(k2, q) * 0.125).reshape(2, F, F))
+        for j in range(4):
+            e = jnp.exp(scores[j] - jnp.max(scores[j], 1, keepdims=True))
+            probs = (e * (1.0 / jnp.sum(e, 1, keepdims=True))).reshape(2 * F, F)
+            pr_s[p * 4 + j] = probs
             v2 = split_heads(qkv_s[rows, 2 * C + j * 128:2 * C + j * 128 + 128])
-            s = (nt(k2, q) * 0.125).reshape(2, F, F)
-            e = jnp.exp(s - jnp.max(s, 1, keepdims=True))
-            probs = (e / jnp.sum(e, 1, keepdims=True)).reshape(2 * F, F)
-            pr_s[p * 4 + j] = probs
-            att_s[rows, j * 128:j * 128 + 128] = tn(probs.astype(BF), v2).astype(BF)
+            at_s[p // 4, j * 128:j * 128 + 128, cols] = tn(v2, probs.astype(BF)).astype(BF)
 
     for h in range(2):
         arrived(rl, h, h)
@@ -210,23 +216,34 @@
         by_pixel(ru, up_s, h)
         da_s[rows, :] = nt(up_s[rows, :], wo[...]).astype(BF)
 
+    def backward_valued(p):
+        rows = pl.ds(pl.multiple_of(p * F, F), F)
+        for j in range(4):
+            da = da_s[rows, j * 128:j * 128 + 128]
+            dv = join_heads(nn(pr_s[p * 4 + j].astype(BF), da)).astype(BF)
+            dqkv_s[rows, 2 * C + j * 128:2 * C + j * 128 + 128] = dv
+
     def backward_attend(p):
         rows = pl.ds(pl.multiple_of(p * F, F), F)
+        lanes = [slice(j * 128, j * 128 + 128) for j in range(4)]
+        da = [da_s[rows, ln] for ln in lanes]
+        probs = [pr_s[p * 4 + j] for j in range(4)]
+        dp = [
+            nt(split_heads(qkv_s[rows, 2 * C + j * 128:2 * C + j * 128 + 128]), da[j])
+            for j in range(4)
+        ]
+        ds = []
         for j in range(4):
-            lanes = slice(j * 128, j * 128 + 128)
-            q = qkv_s[rows, j * 128:j * 128 + 128]
+            p3, d3 = probs[j].reshape(2, F, F), dp[j].reshape(2, F, F)
+            d = p3 * (d3 - jnp.sum(p3 * d3, 1, keepdims=True)) * 0.125
+            ds.append(d.reshape(2 * F, F).astype(BF))
+        for j in range(4):
+            q = qkv_s[rows, lanes[j]]
+            dk = join_heads(nn(ds[j], q)).astype(BF)
+            dqkv_s[rows, C + j * 128:C + j * 128 + 128] = dk
+        for j in range(4):
             k2 = split_heads(qkv_s[rows, C + j * 128:C + j * 128 + 128])
-            v2 = split_heads(qkv_s[rows, 2 * C + j * 128:2 * C + j * 128 + 128])
-            da = da_s[rows, lanes]
-            probs = pr_s[p * 4 + j]
-            dp = nt(v2, da)
-            dv = join_heads(nn(probs.astype(BF), da))
-            p3, d3 = probs.reshape(2, F, F), dp.reshape(2, F, F)
-            ds = p3 * (d3 - jnp.sum(p3 * d3, 1, keepdims=True)) * 0.125
-            ds = ds.reshape(2 * F, F).astype(BF)
-            dqkv_s[rows, j * 128:j * 128 + 128] = tn(ds, k2).astype(BF)
-            dqkv_s[rows, C + j * 128:C + j * 128 + 128] = join_heads(nn(ds, q)).astype(BF)
-            dqkv_s[rows, 2 * C + j * 128:2 * C + j * 128 + 128] = dv.astype(BF)
+            dqkv_s[rows, lanes[j]] = tn(ds[j], k2).astype(BF)
 
     def put(i, h, value):
         value = value.reshape(16, 2, 16, C)
@@ -235,21 +252,16 @@
         else:
             g_s[i] = g_s[i] + value
 
-    def grads_out(h):
-        rows = pl.ds(h * 512, 512)
-        put(6, h, tn(att_s[rows, :], up_s[rows, :]))
-
-    def grads_first(h):
-        rows = pl.ds(h * 512, 512)
-        for i in range(3):
-            put(3 + i, h, tn(nrm_s[rows, :], dqkv_s[rows, i * C:(i + 1) * C]))
-
-    def grads_taps(h):
-        rows = pl.ds(h * 512, 512)
-        for i in range(3):
-            put(i, h, tn(x_s[rows, :], dm_s[rows, i * C:(i + 1) * C]))
-
-    def backward_dense(h):
+    def grad_outer(h):
+        put(6, h, nn(at_s[h], up_s[pl.ds(h * 512, 512), :]))
+
+    def grad_weight(i, h):
+        put(3 + i, h, nn(nt_s[h], dqkv_s[pl.ds(h * 512, 512), i * C:(i + 1) * C]))
+
+    def grad_tap(i, h):
+        put(i, h, nn(xt_s[h], dm_s[pl.ds(h * 512, 512), i * C:(i + 1) * C]))
+
+    def backward_norm(h):
         base = h * 512
         rows = pl.ds(base, 512)
         d_normed = nt(dqkv_s[rows, 0:C], wq[...])
@@ -271,10 +283,13 @@
         dm_s[rows, 0:C] = jnp.where(frame == F - 1, 0.0, pltpu.roll(wide, 511, 0)).astype(BF)
         dm_s[rows, C:2 * C] = d_mid
         dm_s[rows, 2 * C:3 * C] = jnp.where(frame == 0, 0.0, pltpu.roll(wide, 1, 0)).astype(BF)
+
+    def backward_conv(h):
+        rows = pl.ds(h * 512, 512)
         back = nt(dm_s[rows, 0:C], wc[0])
         back = back + nt(dm_s[rows, C:2 * C], wc[1])
         back = back + nt(dm_s[rows, 2 * C:3 * C], wc[2])
-        grad = wide + back
+        grad = dm_s[rows, C:2 * C].astype(F32) + back
         for p in range(4):
             for i in range(4):
                 t32[i, pl.ds(p, F, stride=4), :] = (
@@ -399,42 +414,42 @@
     def gain_cores():
         gn_s[...] = jnp.concatenate(
             [gain_s[:, i * 128:(i + 1) * 128] for i in range(4)] + [jnp.zeros((4, 128), F32)], 0)
-        send(gn_s, gn0, ssem.at[27], rsem.at[27], sib)
+        send(gn_s, gn0, ssem.at[GS], rsem.at[GS], sib)
 
     def gain_x():
-        wait_bytes(gn0, rsem.at[27])
+        wait_bytes(gn0, rsem.at[GS])
         gnx[x] = gn_s[...] + gn0[...]
 
         @pl.loop(1, 4)
         def _(k):
-            send(gnx.at[x], gnx.at[x], ssem.at[28], rsem.at[28], to_x((x + k) % 4))
+            send(gnx.at[x], gnx.at[x], ssem.at[GS + 1], rsem.at[GS + 1], to_x((x + k) % 4))
 
     def gain_y():
-        wait_bytes(gnx.at[pl.ds(0, 3)], rsem.at[28])
+        wait_bytes(gnx.at[pl.ds(0, 3)], rsem.at[GS + 1])
         gny[y] = gnx[0] + gnx[1] + gnx[2] + gnx[3]
 
         @pl.loop(1, 4)
         def _(k):
-            send(gny.at[y], gny.at[y], ssem.at[29], rsem.at[29], to_y((y + k) % 4))
+            send(gny.at[y], gny.at[y], ssem.at[GS + 2], rsem.at[GS + 2], to_y((y + k) % 4))
 
     def gain_z():
-        wait_bytes(gny.at[pl.ds(0, 3)], rsem.at[29])
+        wait_bytes(gny.at[pl.ds(0, 3)], rsem.at[GS + 2])
         gnz[z] = gny[0] + gny[1] + gny[2] + gny[3]
 
         @pl.loop(1, 8)
         def _(k):
-            send(gnz.at[z], gnz.at[z], ssem.at[30], rsem.at[30], at_z((z + k) % 8, c))
+            send(gnz.at[z], gnz.at[z], ssem.at[GS + 3], rsem.at[GS + 3], at_z((z + k) % 8, c))
 
     def gain_end():
-        wait_bytes(gnz.at[pl.ds(0, 7)], rsem.at[30])
+        wait_bytes(gnz.at[pl.ds(0, 7)], rsem.at[GS + 3])
         acc = gnz[0]
         for k in range(1, 8):
             acc = acc + gnz[k]
         ogain[...] = acc
-        wait_bytes(gn_s, ssem.at[27])
-        wait_bytes(gnx.at[pl.ds(0, 3)], ssem.at[28])
-        wait_bytes(gny.at[pl.ds(0, 3)], ssem.at[29])
-        wait_bytes(gnz.at[pl.ds(0, 7)], ssem.at[30])
+        wait_bytes(gn_s, ssem.at[GS])
+        wait_bytes(gnx.at[pl.ds(0, 3)], ssem.at[GS + 1])
+        wait_bytes(gny.at[pl.ds(0, 3)], ssem.at[GS + 2])
+        wait_bytes(gnz.at[pl.ds(0, 7)], ssem.at[GS + 3])
 
     own_out = [pltpu.make_async_copy(osend.at[h, me], orecv.at[h, me], lsem.at[7 + h])
                for h in range(2)]
@@ -444,18 +459,28 @@
 
     @pl.loop(0, 4)
     def _(p):
+        backward_valued(p)
         backward_attend(p)
 
-    grads_out(0)
-    grads_first(0)
-    backward_dense(0)
-    grads_taps(0)
+    grad_outer(0)
+    for i in range(3):
+        grad_weight(i, 0)
+    backward_norm(0)
+    for i in range(3):
+        grad_tap(i, 0)
+    backward_conv(0)
     scatter(osend, orecv, 0, 4)
     own_out[0].start()
 
     arrived(ru, 1, 3)
     backward_att(1)
-    grads_out(1)
+
+    @pl.loop(4, 8)
+    def _(p):
+        backward_valued(p)
+
+    grad_outer(1)
+    grad_weight(2, 1)
     red_cores(0)
 
     @pl.loop(4, 6)
@@ -468,29 +493,40 @@
     def _(p):
         backward_attend(p)
 
-    grads_first(1)
+    grad_weight(0, 1)
+    grad_weight(1, 1)
     red_cores(1)
-    red_second(0)
-    backward_dense(1)
+    backward_norm(1)
     red_first(1)
+    grad_tap(0, 1)
+    red_cores(2)
+    grad_tap(1, 1)
+    red_cores(3)
     gain_cores()
+    red_first(2)
+    grad_tap(2, 1)
+    red_cores(4)
+    red_first(3)
+    backward_conv(1)
+    red_first(4)
     scatter(osend, orecv, 1, 5)
     own_out[1].start()
-    grads_taps(1)
-    red_cores(2)
+    red_second(0)
+    gain_x()
+    red_second(1)
+    red_second(2)
     red_z(0)
-    gain_x()
-    red_first(2)
-    red_gather(0)
-    red_second(1)
     gain_y()
-    red_second(2)
+    red_second(3)
     red_z(1)
+    red_second(4)
+    red_z(2)
     gain_z()
-    red_z(2)
-    red_gather(1)
-    red_gather(2)
-    for g in range(3):
+    red_z(3)
+    red_z(4)
+    for g in range(NG):
+        red_gather(g)
+    for g in range(NG):
         red_end(g)
     gain_end()
 
@@ -501,7 +537,7 @@
         wait_bytes(ref.at[i % 2, pl.ds(0, TM - 1)], ssem.at[i])
 
 
-def finish(orecv, og0, og1, og2, ogain, out, conv, query, key, value, outer, gain):
+def finish(orecv, og0, og1, og2, og3, og4, ogain, out, conv, query, key, value, outer, gain):
     low = row_of((F, C)) % 8 < 4
     for h in range(2):
         got = [[], [], [], []]
@@ -520,9 +556,11 @@
     for q in range(4):
         lanes = slice(q * 128, q * 128 + 128)
         outer[:, lanes] = og0[q, 0].astype(F32)
-        for i, ref in enumerate((query, key, value)):
-            ref[:, lanes] = og1[q, i].astype(F32)
-        conv[:, :, lanes] = og2[q].astype(F32)
+        value[:, lanes] = og0[q, 1].astype(F32)
+        query[:, lanes] = og1[q, 0].astype(F32)
+        key[:, lanes] = og1[q, 1].astype(F32)
+        for i, ref in enumerate((og2, og3, og4)):
+            conv[i, :, lanes] = ref[q, 0].astype(F32)
     tm = lax.axis_index("tm")
     row = ogain[pl.ds(tm // 8, 1), :]
     gain[...] = pltpu.roll(row, (128 - (tm % 8) * 16) % 128, 1)[0, :16]
@@ -534,8 +572,9 @@
         v((4, 256, C)), v((4, 256, C)), v((3, C, C)), v((C, C)), v((C, C)), v((C, C)), v((C, C)),
         v((2, TM, 16, C)), v((2, TM, 16, C)), v((2, TM, 16, C)), v((2, TM, 16, C)),
         v((2, TM, 16, C)),
-        v((4, 512, 128), F32), v((1024, C)), v((1024, C)), v((1024, C)), v((1024, 3 * C)),
-        v((32, 256, F), F32), v((1024, C)), v((1024, C)), v((1024, C)),
+        v((4, 512, 128), F32), v((1024, C)), v((1024, C)),
+        v((2, C, 512)), v((2, C, 512)), v((2, C, 512)), v((1024, 3 * C)),
+        v((32, 256, F), F32), v((1024, C)), v((1024, C)),
         v((1024, 3 * C)), v((1024, 3 * C)),
         v((7, 16, 2, 16, C), F32), v((1, C), F32),
         v((8, 128), F32), v((8, 128), F32), v((4, 8, 128), F32), v((4, 8, 128), F32),
@@ -545,7 +584,7 @@
         n = len(group)
         scratch += [v((16, n, 16, C))] * 2 + [v((4, 4, n, 16, 256))] * 4
         scratch += [v((4, n, 16, 256))] * 4 + [v((4, n, 16, 128)), v((8, n, 16, 128))]
-    scratch += [pltpu.SemaphoreType.DMA((31,)), pltpu.SemaphoreType.DMA((31,)),
+    scratch += [pltpu.SemaphoreType.DMA((GS + 4,)), pltpu.SemaphoreType.DMA((GS + 4,)),
                 pltpu.SemaphoreType.DMA((9,))]
     vmem = pl.BlockSpec(memory_space=pltpu.VMEM)
     hbm = pl.BlockSpec(memory_space=pl.ANY)
@@ -553,13 +592,11 @@
         kernel,
         out_shape=(
             jax.ShapeDtypeStruct((2, TM, 16, C), BF),
-            jax.ShapeDtypeStruct((4, 1, 16, 128), BF),
-            jax.ShapeDtypeStruct((4, 3, 16, 128), BF),
-            jax.ShapeDtypeStruct((4, 3, 16, 128), BF),
+            *[jax.ShapeDtypeStruct((4, len(g), 16, 128), BF) for g in GROUPS],
             jax.ShapeDtypeStruct((8, 128), F32),
         ),
         in_specs=[hbm] * 7 + [vmem],
-        out_specs=(hbm, vmem, vmem, vmem, vmem),
+        out_specs=(hbm, *[vmem] * (NG + 1)),
         scratch_shapes=scratch,
         compiler_params=pltpu.CompilerParams(
             collective_id=0, has_side_effects=True, vmem_limit_bytes=60 * 2**20
@@ -575,7 +612,7 @@
             rows, rows, rows, rows,
             jax.ShapeDtypeStruct((16,), F32),
         ),
-        in_specs=[vmem] * 5,
+        in_specs=[vmem] * (NG + 2),
         out_specs=(vmem,) * 7,
         name="finish",
     )(*got)

time: 115 us -> 112 us (0.974)
  Pallas kernels: 114 us -> 111 us
    pallas_call x1, Pallas kernels: 111 us -> 108 us  [block(): pl.pallas_call(kernel, out_shape=(jax.ShapeDtypeStruct((2, TM, 16, C), BF...]
where the time goes in v3:
time: 112 us
  Pallas kernels  111 us (99%)
    pallas_call x1, Pallas kernels, block(): pl.pallas_call(kernel, out_shape=(jax.ShapeDtypeStruct((2, TM, 16, C), BF...  108 us
    pallas_call x1, Pallas kernels, block(): pl.pallas_call(finish, out_shape=(jax.ShapeDtypeStruct((4, 256, C), BF),...  2.95 us

profile of v3, /device:TPU:1, one launch (start us, length us, event | category | flops | bytes accessed | tf_op | source)
XLA Modules:
  0.0 112.0 jit_solution(13713579340701028417)
XLA Ops:
  0.6 108.4 %block_backward.1 = (bf16[2,32,16,512]{3,2,1,0:T(8,128)(2,1)}, bf16[4,2,16,128]{3,2,1,0:T(8,128)(2,1)}, bf16[4,2,16,128]{3,2,1,0:T(8,128)(2,1)}, bf16[4,1,16,128...) custom-call(bf16[4,256,512]{2,1,0:T(8,128)(2,1)} %bitcast.4, ...), custom_call_target="tpu_custom_call" | custom-call | tf_op jit(solution)/shard_map/block_backward/pallas_call | solution.py:591
  109.0 3.0 %finish.1 = (bf16[4,256,512]{2,1,0:T(8,128)(2,1)}, f32[3,16,512]{2,1,0:T(8,128)}, f32[16,512]{1,0:T(8,128)}, f32[16,512]{1,0:T(8,128)}, f32[16,512]{1,0:T(8,128)}, /*index=5*/f32[16,512]{1,0:T(8,128)}, f32[16]{0:T(128)}) custom-call(bf16[2,32,16,512]{3,2,1,0:T(8,128)(2,1)} %get-tuple-element.21.orecv, bf16[4,2,16,128]{3,2,1,0:T(8,128)(2,1)} %get-tuple-element.22.og0, ...), custom_call_target="tpu_custom_call" | custom-call | tf_op jit(solution)/shard_map/finish/pallas_call | solution.py:607

commit v4 on v3

--- a/solution.py
+++ b/solution.py
@@ -129,8 +129,8 @@
                     [tiles[0][o][m], tiles[1][o][m]], 0
                 ).astype(BF)
 
-    def scatter(src, dst, h, i, lo=1, hi=TM):
-        @pl.loop(lo, hi)
+    def scatter(src, dst, h, i, lo=1, step=1):
+        @pl.loop(lo, TM, step=step)
         def _(k):
             to = (me + k) % TM
             send(src.at[h, to], dst.at[h, me], ssem.at[i], rsem.at[i],
@@ -509,8 +509,7 @@
     red_first(3)
     backward_conv(1)
     red_first(4)
-    scatter(osend, orecv, 1, 5)
-    own_out[1].start()
+    scatter(osend, orecv, 1, 5, 1, 2)
     red_second(0)
     gain_x()
     red_second(1)
@@ -524,6 +523,8 @@
     gain_z()
     red_z(3)
     red_z(4)
+    scatter(osend, orecv, 1, 5, 2, 2)
+    own_out[1].start()
     for g in range(NG):
         red_gather(g)
     for g in range(NG):

time: 112 us -> 109 us (0.973)
  Pallas kernels: 111 us -> 109 us
    pallas_call x1, Pallas kernels: 108 us -> 106 us  [block(): pl.pallas_call(kernel, out_shape=(jax.ShapeDtypeStruct((2, TM, 16, C), BF...]
where the time goes in v4:
time: 109 us
  Pallas kernels  109 us (100%)
    pallas_call x1, Pallas kernels, block(): pl.pallas_call(kernel, out_shape=(jax.ShapeDtypeStruct((2, TM, 16, C), BF...  106 us
    pallas_call x1, Pallas kernels, block(): pl.pallas_call(finish, out_shape=(jax.ShapeDtypeStruct((4, 256, C), BF),...  2.95 us

profile of v4, /device:TPU:1, one launch (start us, length us, event | category | flops | bytes accessed | tf_op | source)
XLA Modules:
  0.0 109.4 jit_solution(1916878315212310585)
XLA Ops:
  0.6 105.8 %block_backward.1 = (bf16[2,32,16,512]{3,2,1,0:T(8,128)(2,1)}, bf16[4,2,16,128]{3,2,1,0:T(8,128)(2,1)}, bf16[4,2,16,128]{3,2,1,0:T(8,128)(2,1)}, bf16[4,1,16,128...) custom-call(bf16[4,256,512]{2,1,0:T(8,128)(2,1)} %bitcast.4, ...), custom_call_target="tpu_custom_call" | custom-call | tf_op jit(solution)/shard_map/block_backward/pallas_call | solution.py:592
  106.4 3.0 %finish.1 = (bf16[4,256,512]{2,1,0:T(8,128)(2,1)}, f32[3,16,512]{2,1,0:T(8,128)}, f32[16,512]{1,0:T(8,128)}, f32[16,512]{1,0:T(8,128)}, f32[16,512]{1,0:T(8,128)}, /*index=5*/f32[16,512]{1,0:T(8,128)}, f32[16]{0:T(128)}) custom-call(bf16[2,32,16,512]{3,2,1,0:T(8,128)(2,1)} %get-tuple-element.21.orecv, bf16[4,2,16,128]{3,2,1,0:T(8,128)(2,1)} %get-tuple-element.22.og0, ...), custom_call_target="tpu_custom_call" | custom-call | tf_op jit(solution)/shard_map/finish/pallas_call | solution.py:608
